TPU v7x, 32 devices: a whole 2x2x4 slice. The times are simulated.
32 devices in a mesh: grp: 2 (over x), ctx: 4 (over y, core), head: 4 (over z).
Axes of the slice: x: 2, y: 2, z: 4, core: 2. Of those that a mesh axis runs over, the one named last changes fastest.
Arguments:
- queries: bfloat16 [4096, 1024], P(('grp', 'ctx'), 'head'), parts along dimension 0, may hold values from -8 to 8
- keys: bfloat16 [4096, 1024], P(('grp', 'ctx'), 'head'), parts along dimension 0, may hold values from -8 to 8
- values: bfloat16 [4096, 1024], P(('grp', 'ctx'), 'head'), parts along dimension 0, may hold values from -6 to 6
- grad_out: bfloat16 [4096, 1024], P(('grp', 'ctx'), 'head'), parts along dimension 0, may hold values from -96 to 96
- block_docs: int32 [32], P('grp'), parts along dimension 0, may hold values from 0 to 7, never falling along the last dimension, each value on 1 to 6 neighbouring positions
- block_order: int32 [32], P('grp'), parts along dimension 0, may hold values from 0 to 15, as said below
Outputs:
- grad_queries: bfloat16 [4096, 1024], P(('grp', 'ctx'), 'head'), parts along dimension 0
- grad_keys: bfloat16 [4096, 1024], P(('grp', 'ctx'), 'head'), parts along dimension 0
- grad_values: bfloat16 [4096, 1024], P(('grp', 'ctx'), 'head'), parts along dimension 0
There are 2 independent parts, one for each index of `grp`. A program takes and returns all parts, laid end to end along the dimension named above; each array names one. Nothing has to cross between parts.
Inputs may be any that keep to these rules, and one draw needn't show every extreme that they name: `block_docs`: never falling along the pack; every shot covers 1 to 6 blocks, one exactly 6. `block_order`: every block exactly once; the 4 positions p with the same p // 4 take at most 1 blocks b with the same b // 4, and some such pair takes exactly 1.
All inputs are finite; a program needn't handle non-finite values.
Results may differ from a plain program's by a relative error of at most 0.0092.
Values may be sent and summed in bfloat16 or wider, within the bound.
No kernel may reach another device: no remote copies, remote signals or barrier semaphores. Data moves between devices by JAX's collectives and lax.ppermute only.
A program may use at most 64 MiB of HBM per device.

v0:
```python
import functools

import jax
import jax.numpy as jnp
import numpy as np
from jax import lax
from jax.experimental import pallas as pl
from jax.experimental.pallas import tpu as pltpu
from jax.sharding import PartitionSpec as P

HEAD_DIM = 128
BLOCK = 128
ARRAYS = 4
NEG_FILL = -1e30
SCALE = HEAD_DIM**-0.5
EXP2_SCALE = SCALE * float(np.log2(np.e))
NT = (((1,), (1,)), ((), ()))
TN = (((0,), (0,)), ((), ()))
NN = (((1,), (0,)), ((), ()))
ANY = pl.BlockSpec(memory_space=pl.ANY)
VMEM = pl.BlockSpec(memory_space=pltpu.VMEM)
SMEM = pl.BlockSpec(memory_space=pltpu.SMEM)


def dot(a, b, dims):
    return lax.dot_general(a, b, dims, preferred_element_type=jnp.float32)


def position_of(order, device, group):
    place = jnp.int32(0)
    block = jnp.int32(0)
    for j in range(4):
        candidate = order[device * 4 + j]
        hit = candidate // 4 == group
        place = jnp.where(hit, j, place)
        block = jnp.where(hit, candidate, block)
    return place, block


def slot_group(device, slot):
    return jnp.where(device // 2 == 0, (2, 3, 1)[slot], (1, 0, 2)[slot])


def far_block(device):
    return jnp.where(device // 2 == 0, 3, 12)


def rows_of(block):
    return pl.ds(pl.multiple_of(block * BLOCK, BLOCK), BLOCK)


def columns_of(head):
    return slice(head * HEAD_DIM, (head + 1) * HEAD_DIM)


def needed(docs, me, block):
    return (docs[block] >= docs[me * 4]) & (docs[block] <= docs[me * 4 + 3])


def pack_slots(order, docs, *refs):
    own, core, outs, held = refs[:3], refs[3:6], refs[6:9], refs[9:]
    me = lax.axis_index("ctx")
    for slot in range(3):
        place, _ = position_of(order, me, slot_group(me, slot))
        for array in range(3):
            outs[slot // 2][slot % 2, array] = own[array][rows_of(place), columns_of(0)]
            outs[2][slot, array] = own[array][rows_of(place), columns_of(1)]
    for sources, device in ((own, me), (core, me ^ 1)):
        for j in range(4):
            block = order[device * 4 + j]
            rows = slice(j * BLOCK, (j + 1) * BLOCK)
            for head in range(2):

                @pl.when((block == far_block(me)) & (me % 2 == head))
                def _(sources=sources, rows=rows, head=head):
                    for array in range(3):
                        outs[1][1, array] = sources[array][rows, columns_of(head)]

            @pl.when(needed(docs, me, block))
            def _(sources=sources, rows=rows, block=block):
                for array in range(3):
                    for head in range(2):
                        held[head][array, rows_of(block), :] = sources[array][rows, columns_of(head)]


def one_doc(length, exact, start, end, base, blocks, keys_held, held, prob, dsc, results):
    window = start if exact else jnp.minimum(start, blocks - length)
    rows = length * BLOCK
    whole = pl.ds(pl.multiple_of(window * BLOCK, BLOCK), rows)
    keys = keys_held[whole, :]
    values = held[0, whole, :]
    pair = min(3 if exact and length != 4 else 2, length)
    if not exact:
        key_block = window + lax.broadcasted_iota(jnp.int32, (rows, pair * BLOCK), 0) // BLOCK
        key_ok = (key_block >= start) & (key_block < end)

    def stats(first):
        at = window + first
        these = pl.ds(pl.multiple_of(at * BLOCK, BLOCK), pair * BLOCK)
        queries = held[1, these, :]
        douts = held[2, these, :]
        scores = dot(keys, queries, NT) * EXP2_SCALE
        dprob = dot(values, douts, NT)
        if not exact:
            scores = jnp.where(key_ok, scores, NEG_FILL)
        top = jnp.max(scores, axis=0, keepdims=True)
        weights = jnp.exp2(scores - top)
        inverse = 1.0 / jnp.sum(weights, axis=0, keepdims=True)
        probabilities = weights * inverse
        delta = jnp.sum(probabilities * dprob, axis=0, keepdims=True)
        dscore = probabilities * (dprob - delta)
        if not exact:
            query_block = at + lax.broadcasted_iota(jnp.int32, (rows, pair * BLOCK), 1) // BLOCK
            ok = key_ok & (query_block >= start) & (query_block < end)
            probabilities = jnp.where(ok, probabilities, 0.0)
            dscore = jnp.where(ok, dscore, 0.0)
        return probabilities.astype(jnp.bfloat16), dscore.astype(jnp.bfloat16)

    queries = held[1, whole, :]
    douts = held[2, whole, :]

    def store(first, count, prob_rows, dsc_rows, dsc_columns):
        def put(array, value):
            results.stage[array, results.rows(first - base, count), :] = value.astype(jnp.bfloat16)
            results.copy(array, first - base, count).start()

        put(2, dot(prob_rows, douts, NN))
        put(1, dot(dsc_rows, queries, NN) * SCALE)
        put(0, dot(dsc_columns, keys, TN) * SCALE)

    if exact and length <= 2:
        prob_low, dsc_low = stats(0)
        for i in range(length):
            mine = slice(i * BLOCK, (i + 1) * BLOCK)
            block = start + i
            pl.when((block >= base) & (block < base + 4))(
                functools.partial(store, block, 1, prob_low[mine], dsc_low[mine], dsc_low[:, mine])
            )
        return

    def fill(step, carry):
        first = jnp.minimum(step * pair, length - pair)
        columns = pl.ds(pl.multiple_of(first * BLOCK, BLOCK), pair * BLOCK)
        prob[0:rows, columns], dsc[0:rows, columns] = stats(first)
        return carry

    lax.fori_loop(0, -(-length // pair), fill, 0)
    first = jnp.maximum(start, base)
    owned = jnp.minimum(end, base + 4) - first
    mine = pl.multiple_of((first - window) * BLOCK, BLOCK)
    for count in range(1, min(4, length) + 1):

        @pl.when(owned == count)
        def _(count=count):
            these = pl.ds(mine, count * BLOCK)
            store(first, count, prob[these, 0:rows], dsc[these, 0:rows], dsc[0:rows, these])


class Results:
    def __init__(self, head, outs, stage, sems):
        self.head, self.outs, self.stage, self.sems = head, outs, stage, sems

    def rows(self, at, count):
        return pl.ds(pl.multiple_of(at * BLOCK, BLOCK), count * BLOCK)

    def copy(self, array, at, count):
        rows = self.rows(at, count)
        return pltpu.make_async_copy(
            self.stage.at[array, rows, :],
            self.outs[array].at[rows, pl.ds(self.head * HEAD_DIM, HEAD_DIM)],
            self.sems.at[array],
        )


def all_docs(blocks, longest, base, docs, keys_held, held, prob, dsc, results):
    if longest <= 8:
        sizes = list(range(1, longest + 1))
    else:
        step = -(-longest // 6)
        sizes = [min(longest, step * (i + 1)) for i in range(-(-longest // step))]

    def visit(t, carry):
        block = base + t
        doc = docs[block]
        begins = jnp.logical_or(t == 0, docs[jnp.maximum(block - 1, 0)] != doc)

        @pl.when(begins)
        def _():
            start, end = jnp.int32(0), jnp.int32(0)
            for b in range(blocks):
                other = docs[b]
                start += (other < doc).astype(jnp.int32)
                end += (other <= doc).astype(jnp.int32)
            length = end - start
            below = 0
            for size in sizes:
                pl.when((length > below) & (length <= size))(
                    functools.partial(
                        one_doc, size, size - below == 1, start, end, base, blocks, keys_held, held, prob, dsc, results
                    )
                )
                below = size

        return carry

    lax.fori_loop(0, 4, visit, 0)
    for array in range(3):
        results.copy(array, 0, 4).wait()


def attend_slots(blocks, longest, head, order, docs, *refs):
    keys, (far_row, far_diag) = refs[1:5], refs[5:7]
    row, diag = (refs[7:9], refs[9:11]) if head == 0 else (refs[7:8], refs[8:9])
    outs, held, (prob, dsc, stage, sems, keys_held) = refs[-9:-6], refs[-6], refs[-5:]
    me = lax.axis_index("ctx")
    other = me ^ 2

    for flip, source in enumerate(keys):
        for j in range(4):
            block = order[(me ^ flip) * 4 + j]

            @pl.when(needed(docs, me, block))
            def _(source=source, j=j, block=block):
                keys_held[rows_of(block), :] = source[j * BLOCK : (j + 1) * BLOCK, columns_of(head)]

    def bring(block, source, at, also=True):
        @pl.when(needed(docs, me, block) & also)
        def _():
            for array in range(3):
                held[array, rows_of(block), :] = source[at, array]

    for slot in range(3):
        for device, pieces in ((other, row), (other ^ 1, diag)):
            _, block = position_of(order, device, slot_group(device, slot))
            bring(block, pieces[slot // pieces[0].shape[0]], slot % pieces[0].shape[0])
    block = far_block(other)
    held_there = order[other // 2 * 8] == block
    for position in range(1, 8):
        held_there |= order[other // 2 * 8 + position] == block
    for source, core_of in ((far_row, head), (far_diag, 1 - head)):
        bring(block, source, source.shape[0] - 1, held_there & (me % 2 == core_of))

    all_docs(blocks, longest, me * 4, docs, keys_held, held, prob, dsc, Results(head, outs, stage, sems))


def attend_gathered(blocks, longest, head, order, docs, keys, values, queries, grad_out, *rest):
    outs, (prob, dsc, stage, out_sems, keys_held, held, sems) = rest[-10:-7], rest[-7:]
    me = lax.axis_index("ctx")

    def copies(position):
        rows = pl.ds(pl.multiple_of(position * BLOCK, BLOCK), BLOCK)
        to = pl.ds(pl.multiple_of(order[position] * BLOCK, BLOCK), BLOCK)
        return [
            pltpu.make_async_copy(
                source.at[rows, pl.ds(head * HEAD_DIM, HEAD_DIM)],
                keys_held.at[to, :] if array == 0 else held.at[array - 1, to, :],
                sems.at[position * ARRAYS + array],
            )
            for array, source in enumerate((keys, values, queries, grad_out))
        ]

    def begin(position, carry):
        for copy in copies(position):
            copy.start()
        return carry

    def finish(position, carry):
        for copy in copies(position):
            copy.wait()
        return carry

    lax.fori_loop(0, blocks, begin, 0)
    lax.fori_loop(0, blocks, finish, 0)
    results = Results(head, outs, stage, out_sems)
    all_docs(blocks, longest, me * 4, docs, keys_held, held, prob, dsc, results)


def attend(kernel, sources, previous, order, docs, rows, blocks, longest, heads, gathered):
    out_shape = [jax.ShapeDtypeStruct((rows, heads * HEAD_DIM), jnp.bfloat16)] * 3
    out_specs = [ANY] * 3
    held = (ARRAYS - 1, blocks * BLOCK, HEAD_DIM)
    first = 2 + len(sources)
    aliases = {first + i: i for i in range(len(previous))}
    scratch = [
        pltpu.VMEM((longest * BLOCK, longest * BLOCK), jnp.bfloat16),
        pltpu.VMEM((longest * BLOCK, longest * BLOCK), jnp.bfloat16),
        pltpu.VMEM((3, 4 * BLOCK, HEAD_DIM), jnp.bfloat16),
        pltpu.SemaphoreType.DMA((3,)),
        pltpu.VMEM((blocks * BLOCK, HEAD_DIM), jnp.bfloat16),
    ]
    if gathered:
        scratch += [pltpu.VMEM(held, jnp.bfloat16), pltpu.SemaphoreType.DMA((blocks * ARRAYS,))]
    else:
        out_shape.append(jax.ShapeDtypeStruct(held, jnp.bfloat16))
        out_specs.append(VMEM)
        aliases[2] = 3
    return pl.pallas_call(
        kernel,
        out_shape=out_shape,
        in_specs=[SMEM, SMEM] + [ANY if gathered else VMEM] * len(sources) + [ANY] * len(previous),
        out_specs=out_specs,
        scratch_shapes=scratch,
        input_output_aliases=aliases,
        compiler_params=pltpu.CompilerParams(vmem_limit_bytes=(60 if gathered else 32) << 20),
        cost_estimate=pl.CostEstimate(
            flops=10**6, bytes_accessed=10**4, transcendentals=10**3
        ),
        name="attend",
    )(order, docs, *sources, *previous)[:3]


def local(queries, keys, values, grad_out, block_docs, block_order):
    rows, width = queries.shape
    heads = width // HEAD_DIM
    blocks = block_order.shape[0]
    longest = blocks * 3 // 8
    arrays = (keys, values, queries, grad_out)
    grads = ()
    if lax.axis_size("ctx") != 4 or blocks != 16 or heads != 2:
        whole = [lax.all_gather(x, "ctx", axis=0, tiled=True) for x in arrays]
        for head in range(heads):
            grads = attend(
                functools.partial(attend_gathered, blocks, longest, head),
                whole, grads, block_order, block_docs, rows, blocks, longest, heads, True,
            )
        return tuple(grads)

    def swap(array, flip):
        return lax.ppermute(array, "ctx", [(i, i ^ flip) for i in range(4)])

    key_row = swap(keys, 2)
    core = [swap(x, 1) for x in arrays]
    shapes = [(slots, 3, BLOCK, HEAD_DIM) for slots in (2, 2, 3)] + [(3, blocks * BLOCK, HEAD_DIM)] * 2
    *packed, held0, held1 = pl.pallas_call(
        pack_slots,
        out_shape=[jax.ShapeDtypeStruct(shape, jnp.bfloat16) for shape in shapes],
        in_specs=[SMEM] * 2 + [VMEM] * 6,
        out_specs=[VMEM] * 5,
        compiler_params=pltpu.CompilerParams(vmem_limit_bytes=16 << 20),
        name="pack",
    )(block_order, block_docs, *arrays[1:], *core[1:])
    row = [swap(x, 2) for x in packed]
    all_keys = (keys, core[0], key_row, swap(key_row, 1))
    diag = [swap(x, 1) for x in row[:2]]
    far = (row[1], diag[1])
    grads = attend(
        functools.partial(attend_slots, blocks, longest, 0),
        (held0, *all_keys, *far, *row[:2], *diag), (), block_order, block_docs, rows, blocks, longest, heads, False,
    )
    last, grads = lax.optimization_barrier((row[2], grads))
    grads = attend(
        functools.partial(attend_slots, blocks, longest, 1),
        (held1, *all_keys, *far, last, swap(last, 1)), grads, block_order, block_docs, rows, blocks, longest, heads, False,
    )
    return tuple(grads)


def solution(mesh):
    rows = P(("grp", "ctx"), "head")
    return jax.shard_map(
        local,
        mesh=mesh,
        in_specs=(rows, rows, rows, rows, P("grp"), P("grp")),
        out_specs=(rows, rows, rows),
        check_vma=False,
    )
```

profile of v0, /device:TPU:1, one launch (start us, length us, event | category | flops | bytes accessed | tf_op | source)
XLA Modules:
  0.0 34.8 jit_solution(11258841914618373103)
XLA Ops:
  0.6 0.0 copy-start
  0.6 0.1 collective-permute-start.1
  0.8 0.5 %collective-permute-start = (bf16[512,256]{1,0:T(8,128)(2,1)}, bf16[512,256]{1,0:T(8,128)(2,1)S(1)}, u32[]{:S(2)}, u32[]{:S(2)}) collective-permute-start(bf16[512,256]{1,0:T(8,128)(2,1)} %refs_0_.1), channel_id=1, source_target_pairs={{0,4},{4,0},{8,12},{12,8},{1,5},{5,1},{9,13},{13,9},{2,6},{6,2},{1... | collective-permute-start | bytes 786440 | tf_op jit(solution)/shard_map/ppermute | solution.py:329
  1.2 0.1 collective-permute-start.2
  1.3 2.7 %collective-permute-start.4 = (bf16[512,256]{1,0:T(8,128)(2,1)}, bf16[512,256]{1,0:T(8,128)(2,1)S(1)}, u32[]{:S(2)}, u32[]{:S(2)}) collective-permute-start(bf16[512,256]{1,0:T(8,128)(2,1)} %refs_1_.5), channel_id=1, source_target_pairs={{0,8},{4,12},{8,0},{12,4},{1,9},{5,13},{9,1},{13,5},{2,10},{6,14},... | collective-permute-start | bytes 786440 | tf_op jit(solution)/shard_map/ppermute | solution.py:329
  4.0 0.0 collective-permute-done.1.refs_4_
  4.0 0.0 collective-permute-done.refs_3_
  4.0 0.0 collective-permute-done.2.refs_5_
  4.0 0.0 copy-start.1
  4.0 0.9 %copy-done.1 = bf16[512,256]{1,0:T(8,128)(2,1)S(1)} copy-done((bf16[512,256]{1,0:T(8,128)(2,1)S(1)}, bf16[512,256]{1,0:T(8,128)(2,1)}, u32[]{:S(2)}) %copy-start.1) | copy-done | bytes 262168
  4.9 0.0 copy-start.2
  4.9 0.9 %copy-done.2 = bf16[512,256]{1,0:T(8,128)(2,1)S(1)} copy-done((bf16[512,256]{1,0:T(8,128)(2,1)S(1)}, bf16[512,256]{1,0:T(8,128)(2,1)}, u32[]{:S(2)}) %copy-start.2) | copy-done | bytes 262168
  5.9 0.0 copy-start.3
  5.9 0.9 %copy-done.3 = bf16[512,256]{1,0:T(8,128)(2,1)S(1)} copy-done((bf16[512,256]{1,0:T(8,128)(2,1)S(1)}, bf16[512,256]{1,0:T(8,128)(2,1)}, u32[]{:S(2)}) %copy-start.3) | copy-done | bytes 262168
  6.8 0.0 copy-start.4
  6.8 0.7 %copy-done.4 = s32[16]{0:T(128)S(1)} copy-done((s32[16]{0:T(128)S(1)}, s32[16]{0:T(128)}, u32[]{:S(2)}) %copy-start.4) | copy-done | bytes 88
  7.5 0.0 copy-start.6
  7.5 0.7 %copy-done.6 = s32[16]{0:T(128)S(1)} copy-done((s32[16]{0:T(128)S(1)}, s32[16]{0:T(128)}, u32[]{:S(2)}) %copy-start.6) | copy-done | bytes 88
  8.2 0.0 copy-start.5
  8.2 0.0 copy-start.7
  8.2 1.0 %pack.1 = (bf16[2,3,128,128]{3,2,1,0:T(8,128)(2,1)S(1)}, bf16[2,3,128,128]{3,2,1,0:T(8,128)(2,1)S(1)}, bf16[3,3,128,128]{3,2,1,0:T(8,128)(2,1)S(1)}, bf16[3,2048...) custom-call(s32[16]{0:T(128)S(1)} %copy-done.4, s32[16]{0:T(128)S(1)} %copy-done.6, bf16[512,256]{1,0:T(8,128)(2,1)S(1)} %copy-done.1, ...), custom_call_target="tpu_custom_call" | custom-call | tf_op jit(solution)/shard_map/pack/pallas_call | solution.py:334
  9.2 1.6 %collective-permute-start.6 = (bf16[2,3,128,128]{3,2,1,0:T(8,128)(2,1)S(1)}, bf16[2,3,128,128]{3,2,1,0:T(8,128)(2,1)S(1)}, u32[]{:S(2)}, u32[]{:S(2)}) collective-permute-start(bf16[2,3,128,128]{3,2,1,0:T(8,128)(2,1)S(1)} %get-tuple-element.19), channel_id=1, source_target_pairs={{0,8},{4,12},{8,0},{12,4},{1,9},{5,13},{9,1},{13,5},{2,10},{6,14},... | collective-permute-start | bytes 589832 | tf_op jit(solution)/shard_map/ppermute | solution.py:329
  10.8 0.1 collective-permute-start.9
  10.9 1.4 %collective-permute-start.8 = (bf16[3,3,128,128]{3,2,1,0:T(8,128)(2,1)S(1)}, bf16[3,3,128,128]{3,2,1,0:T(8,128)(2,1)S(1)}, u32[]{:S(2)}, u32[]{:S(2)}) collective-permute-start(bf16[3,3,128,128]{3,2,1,0:T(8,128)(2,1)S(1)} %get-tuple-element.20), channel_id=1, source_target_pairs={{0,8},{4,12},{8,0},{12,4},{1,9},{5,13},{9,1},{13,5},{2,10},{6,14},... | collective-permute-start | bytes 884744 | tf_op jit(solution)/shard_map/ppermute | solution.py:329
  12.3 0.0 copy-done
  12.3 1.2 %collective-permute-start.3 = (bf16[512,256]{1,0:T(8,128)(2,1)S(1)}, bf16[512,256]{1,0:T(8,128)(2,1)S(1)}, u32[]{:S(2)}, u32[]{:S(2)}) collective-permute-start(bf16[512,256]{1,0:T(8,128)(2,1)S(1)} %copy-done), channel_id=1, source_target_pairs={{0,4},{4,0},{8,12},{12,8},{1,5},{5,1},{9,13},{13,9},{2,6},{6,2},{1... | collective-permute-start | bytes 786440 | tf_op jit(solution)/shard_map/ppermute | solution.py:329
  13.5 0.0 collective-permute-done.4.refs_3_
  13.5 0.1 collective-permute-start.5
  13.6 2.0 %collective-permute-done.6.refs_5_.refs_8_ = bf16[2,3,128,128]{3,2,1,0:T(8,128)(2,1)S(1)} collective-permute-done((bf16[2,3,128,128]{3,2,1,0:T(8,128)(2,1)S(1)}, bf16[2,3,128,128]{3,2,1,0:T(8,128)(2,1)S(1)}, u32[]{:S(2)}, u32[]{:S(2)}) %collective-permute-start.6) | collective-permute-done | bytes 196640 | tf_op jit(solution)/shard_map/ppermute | solution.py:329
  15.6 1.7 %collective-permute-start.7 = (bf16[2,3,128,128]{3,2,1,0:T(8,128)(2,1)S(1)}, bf16[2,3,128,128]{3,2,1,0:T(8,128)(2,1)S(1)}, u32[]{:S(2)}, u32[]{:S(2)}) collective-permute-start(bf16[2,3,128,128]{3,2,1,0:T(8,128)(2,1)S(1)} %collective-permute-done.6.refs_5_.refs_8_), channel_id=1, source_target_pairs={{0,4},{4,0},{8,12},{12,8},{1,5},{5,1},{9,13},{13,9},{2,6},{6,2},{1... | collective-permute-start | bytes 589832 | tf_op jit(solution)/shard_map/ppermute | solution.py:329
  17.3 2.6 %collective-permute-done.9.refs_7_ = bf16[2,3,128,128]{3,2,1,0:T(8,128)(2,1)S(1)} collective-permute-done((bf16[2,3,128,128]{3,2,1,0:T(8,128)(2,1)S(1)}, bf16[2,3,128,128]{3,2,1,0:T(8,128)(2,1)S(1)}, u32[]{:S(2)}, u32[]{:S(2)}) %collective-permute-start.9) | collective-permute-done | bytes 196640 | tf_op jit(solution)/shard_map/ppermute | solution.py:329
  19.8 1.7 %collective-permute-start.10 = (bf16[2,3,128,128]{3,2,1,0:T(8,128)(2,1)S(1)}, bf16[2,3,128,128]{3,2,1,0:T(8,128)(2,1)S(1)}, u32[]{:S(2)}, u32[]{:S(2)}) collective-permute-start(bf16[2,3,128,128]{3,2,1,0:T(8,128)(2,1)S(1)} %collective-permute-done.9.refs_7_), channel_id=1, source_target_pairs={{0,4},{4,0},{8,12},{12,8},{1,5},{5,1},{9,13},{13,9},{2,6},{6,2},{1... | collective-permute-start | bytes 589832 | tf_op jit(solution)/shard_map/ppermute | solution.py:329
  21.5 0.0 collective-permute-done.3.refs_2_
  21.5 0.0 collective-permute-done.5.refs_4_
  21.5 0.0 collective-permute-done.7.refs_6_.refs_10_
  21.5 1.1 %collective-permute-done.10.refs_9_ = bf16[2,3,128,128]{3,2,1,0:T(8,128)(2,1)S(1)} collective-permute-done((bf16[2,3,128,128]{3,2,1,0:T(8,128)(2,1)S(1)}, bf16[2,3,128,128]{3,2,1,0:T(8,128)(2,1)S(1)}, u32[]{:S(2)}, u32[]{:S(2)}) %collective-permute-start.10) | collective-permute-done | bytes 196640 | tf_op jit(solution)/shard_map/ppermute | solution.py:329
  22.6 0.0 copy-done.5
  22.6 0.0 copy-done.7
  22.6 5.1 %attend.2 = (bf16[512,256]{1,0:T(8,128)(2,1)}, bf16[512,256]{1,0:T(8,128)(2,1)}, bf16[512,256]{1,0:T(8,128)(2,1)}, bf16[3,2048,128]{2,1,0:T(8,128)(2,1)S(1)}) custom-call(s32[16]{0:T(128)S(1)} %copy-done.5, s32[16]{0:T(128)S(1)} %copy-done.7, bf16[3,2048,128]{2,1,0:T(8,128)(2,1)S(1)} %get-tuple-element.21.refs_0_, ...), custom_call_target="tpu_custom_call", output_to_operand_aliasing={{3}: (2, {})} | custom-call | flops 1000000 | bytes 10000 | tf_op jit(solution)/shard_map/attend/pallas_call | solution.py:297
  27.7 0.0 collective-permute-done.8.refs_7_
  27.7 0.1 collective-permute-start.11
  27.8 1.6 %collective-permute-done.11.refs_8_ = bf16[3,3,128,128]{3,2,1,0:T(8,128)(2,1)S(1)} collective-permute-done((bf16[3,3,128,128]{3,2,1,0:T(8,128)(2,1)S(1)}, bf16[3,3,128,128]{3,2,1,0:T(8,128)(2,1)S(1)}, u32[]{:S(2)}, u32[]{:S(2)}) %collective-permute-start.11) | collective-permute-done | bytes 294944 | tf_op jit(solution)/shard_map/ppermute | solution.py:329
  29.4 5.3 %attend.3 = (bf16[512,256]{1,0:T(8,128)(2,1)}, bf16[512,256]{1,0:T(8,128)(2,1)}, bf16[512,256]{1,0:T(8,128)(2,1)}, bf16[3,2048,128]{2,1,0:T(8,128)(2,1)S(1)}) custom-call(s32[16]{0:T(128)S(1)} %copy-done.5, s32[16]{0:T(128)S(1)} %copy-done.7, ...), custom_call_target="tpu_custom_call", output_to_operand_aliasing={{0}: (11, {}), {1}: (12, {}), {2}: (13, {}), {3}: (2, {})} | custom-call | flops 1000000 | bytes 10000 | tf_op jit(solution)/shard_map/attend/pallas_call | solution.py:297
Async XLA Ops:
  0.6 11.6 %copy-start = (bf16[512,256]{1,0:T(8,128)(2,1)S(1)}, bf16[512,256]{1,0:T(8,128)(2,1)}, u32[]{:S(2)}) copy-start(bf16[512,256]{1,0:T(8,128)(2,1)} %refs_1_.5) | copy-start | bytes 786436
  0.6 3.3 %collective-permute-start.1 = (bf16[512,256]{1,0:T(8,128)(2,1)}, bf16[512,256]{1,0:T(8,128)(2,1)S(1)}, u32[]{:S(2)}, u32[]{:S(2)}) collective-permute-start(bf16[512,256]{1,0:T(8,128)(2,1)} %refs_1_.3), channel_id=1, source_target_pairs={{0,4},{4,0},{8,12},{12,8},{1,5},{5,1},{9,13},{13,9},{2,6},{6,2},{1... | collective-permute-start | bytes 786440 | tf_op jit(solution)/shard_map/ppermute | solution.py:329
  0.8 3.2 %collective-permute-start = (bf16[512,256]{1,0:T(8,128)(2,1)}, bf16[512,256]{1,0:T(8,128)(2,1)S(1)}, u32[]{:S(2)}, u32[]{:S(2)}) collective-permute-start(bf16[512,256]{1,0:T(8,128)(2,1)} %refs_0_.1), channel_id=1, source_target_pairs={{0,4},{4,0},{8,12},{12,8},{1,5},{5,1},{9,13},{13,9},{2,6},{6,2},{1... | collective-permute-start | bytes 786440 | tf_op jit(solution)/shard_map/ppermute | solution.py:329
  1.2 2.8 %collective-permute-start.2 = (bf16[512,256]{1,0:T(8,128)(2,1)}, bf16[512,256]{1,0:T(8,128)(2,1)S(1)}, u32[]{:S(2)}, u32[]{:S(2)}) collective-permute-start(bf16[512,256]{1,0:T(8,128)(2,1)} %refs_2_.1), channel_id=1, source_target_pairs={{0,4},{4,0},{8,12},{12,8},{1,5},{5,1},{9,13},{13,9},{2,6},{6,2},{1... | collective-permute-start | bytes 786440 | tf_op jit(solution)/shard_map/ppermute | solution.py:329
  1.3 12.2 %collective-permute-start.4 = (bf16[512,256]{1,0:T(8,128)(2,1)}, bf16[512,256]{1,0:T(8,128)(2,1)S(1)}, u32[]{:S(2)}, u32[]{:S(2)}) collective-permute-start(bf16[512,256]{1,0:T(8,128)(2,1)} %refs_1_.5), channel_id=1, source_target_pairs={{0,8},{4,12},{8,0},{12,4},{1,9},{5,13},{9,1},{13,5},{2,10},{6,14},... | collective-permute-start | bytes 786440 | tf_op jit(solution)/shard_map/ppermute | solution.py:329
  4.0 1.0 %copy-start.1 = (bf16[512,256]{1,0:T(8,128)(2,1)S(1)}, bf16[512,256]{1,0:T(8,128)(2,1)}, u32[]{:S(2)}) copy-start(bf16[512,256]{1,0:T(8,128)(2,1)} %refs_0_.1) | copy-start | bytes 786436
  4.9 0.9 %copy-start.2 = (bf16[512,256]{1,0:T(8,128)(2,1)S(1)}, bf16[512,256]{1,0:T(8,128)(2,1)}, u32[]{:S(2)}) copy-start(bf16[512,256]{1,0:T(8,128)(2,1)} %refs_1_.3) | copy-start | bytes 786436
  5.9 0.9 %copy-start.3 = (bf16[512,256]{1,0:T(8,128)(2,1)S(1)}, bf16[512,256]{1,0:T(8,128)(2,1)}, u32[]{:S(2)}) copy-start(bf16[512,256]{1,0:T(8,128)(2,1)} %refs_2_.1) | copy-start | bytes 786436
  6.8 0.7 %copy-start.4 = (s32[16]{0:T(128)S(1)}, s32[16]{0:T(128)}, u32[]{:S(2)}) copy-start(s32[16]{0:T(128)} %order.5) | copy-start | bytes 196
  7.5 0.7 %copy-start.6 = (s32[16]{0:T(128)S(1)}, s32[16]{0:T(128)}, u32[]{:S(2)}) copy-start(s32[16]{0:T(128)} %docs.5) | copy-start | bytes 196
  8.2 14.4 %copy-start.5 = (s32[16]{0:T(128)S(1)}, s32[16]{0:T(128)}, u32[]{:S(2)}) copy-start(s32[16]{0:T(128)} %order.5) | copy-start | bytes 196
  8.2 14.4 %copy-start.7 = (s32[16]{0:T(128)S(1)}, s32[16]{0:T(128)}, u32[]{:S(2)}) copy-start(s32[16]{0:T(128)} %docs.5) | copy-start | bytes 196
  9.2 6.4 %collective-permute-start.6 = (bf16[2,3,128,128]{3,2,1,0:T(8,128)(2,1)S(1)}, bf16[2,3,128,128]{3,2,1,0:T(8,128)(2,1)S(1)}, u32[]{:S(2)}, u32[]{:S(2)}) collective-permute-start(bf16[2,3,128,128]{3,2,1,0:T(8,128)(2,1)S(1)} %get-tuple-element.19), channel_id=1, source_target_pairs={{0,8},{4,12},{8,0},{12,4},{1,9},{5,13},{9,1},{13,5},{2,10},{6,14},... | collective-permute-start | bytes 589832 | tf_op jit(solution)/shard_map/ppermute | solution.py:329
  10.8 9.0 %collective-permute-start.9 = (bf16[2,3,128,128]{3,2,1,0:T(8,128)(2,1)S(1)}, bf16[2,3,128,128]{3,2,1,0:T(8,128)(2,1)S(1)}, u32[]{:S(2)}, u32[]{:S(2)}) collective-permute-start(bf16[2,3,128,128]{3,2,1,0:T(8,128)(2,1)S(1)} %get-tuple-element.22), channel_id=1, source_target_pairs={{0,8},{4,12},{8,0},{12,4},{1,9},{5,13},{9,1},{13,5},{2,10},{6,14},... | collective-permute-start | bytes 589832 | tf_op jit(solution)/shard_map/ppermute | solution.py:329
  10.9 16.8 %collective-permute-start.8 = (bf16[3,3,128,128]{3,2,1,0:T(8,128)(2,1)S(1)}, bf16[3,3,128,128]{3,2,1,0:T(8,128)(2,1)S(1)}, u32[]{:S(2)}, u32[]{:S(2)}) collective-permute-start(bf16[3,3,128,128]{3,2,1,0:T(8,128)(2,1)S(1)} %get-tuple-element.20), channel_id=1, source_target_pairs={{0,8},{4,12},{8,0},{12,4},{1,9},{5,13},{9,1},{13,5},{2,10},{6,14},... | collective-permute-start | bytes 884744 | tf_op jit(solution)/shard_map/ppermute | solution.py:329
  12.3 9.2 %collective-permute-start.3 = (bf16[512,256]{1,0:T(8,128)(2,1)S(1)}, bf16[512,256]{1,0:T(8,128)(2,1)S(1)}, u32[]{:S(2)}, u32[]{:S(2)}) collective-permute-start(bf16[512,256]{1,0:T(8,128)(2,1)S(1)} %copy-done), channel_id=1, source_target_pairs={{0,4},{4,0},{8,12},{12,8},{1,5},{5,1},{9,13},{13,9},{2,6},{6,2},{1... | collective-permute-start | bytes 786440 | tf_op jit(solution)/shard_map/ppermute | solution.py:329
  13.5 8.0 %collective-permute-start.5 = (bf16[512,256]{1,0:T(8,128)(2,1)S(1)}, bf16[512,256]{1,0:T(8,128)(2,1)S(1)}, u32[]{:S(2)}, u32[]{:S(2)}) collective-permute-start(bf16[512,256]{1,0:T(8,128)(2,1)S(1)} %collective-permute-done.4.refs_3_), channel_id=1, source_target_pairs={{0,4},{4,0},{8,12},{12,8},{1,5},{5,1},{9,13},{13,9},{2,6},{6,2},{1... | collective-permute-start | bytes 786440 | tf_op jit(solution)/shard_map/ppermute | solution.py:329
  15.6 5.9 %collective-permute-start.7 = (bf16[2,3,128,128]{3,2,1,0:T(8,128)(2,1)S(1)}, bf16[2,3,128,128]{3,2,1,0:T(8,128)(2,1)S(1)}, u32[]{:S(2)}, u32[]{:S(2)}) collective-permute-start(bf16[2,3,128,128]{3,2,1,0:T(8,128)(2,1)S(1)} %collective-permute-done.6.refs_5_.refs_8_), channel_id=1, source_target_pairs={{0,4},{4,0},{8,12},{12,8},{1,5},{5,1},{9,13},{13,9},{2,6},{6,2},{1... | collective-permute-start | bytes 589832 | tf_op jit(solution)/shard_map/ppermute | solution.py:329
  19.8 2.7 %collective-permute-start.10 = (bf16[2,3,128,128]{3,2,1,0:T(8,128)(2,1)S(1)}, bf16[2,3,128,128]{3,2,1,0:T(8,128)(2,1)S(1)}, u32[]{:S(2)}, u32[]{:S(2)}) collective-permute-start(bf16[2,3,128,128]{3,2,1,0:T(8,128)(2,1)S(1)} %collective-permute-done.9.refs_7_), channel_id=1, source_target_pairs={{0,4},{4,0},{8,12},{12,8},{1,5},{5,1},{9,13},{13,9},{2,6},{6,2},{1... | collective-permute-start | bytes 589832 | tf_op jit(solution)/shard_map/ppermute | solution.py:329
  27.7 1.6 %collective-permute-start.11 = (bf16[3,3,128,128]{3,2,1,0:T(8,128)(2,1)S(1)}, bf16[3,3,128,128]{3,2,1,0:T(8,128)(2,1)S(1)}, u32[]{:S(2)}, u32[]{:S(2)}) collective-permute-start(bf16[3,3,128,128]{3,2,1,0:T(8,128)(2,1)S(1)} %collective-permute-done.8.refs_7_), channel_id=1, source_target_pairs={{0,4},{4,0},{8,12},{12,8},{1,5},{5,1},{9,13},{13,9},{2,6},{6,2},{1... | collective-permute-start | bytes 884744 | tf_op jit(solution)/shard_map/ppermute | solution.py:329
where the time goes:
time: 34.9 us; the launch traced here: 34.8 us
  Pallas kernels  11.5 us (33%)
  starting transfers between devices  11.1 us (32%)
  waiting for transfers between devices  7.25 us (21%)
  local copies, waits for them, and re-layouts  4.16 us (12%)
  between operations  0.86 us (2%)
    ppermute x12, starting transfers between devices, swap(): return lax.ppermute(array, 'ctx', [(i, i ^ flip) for i in range(4)])  11.1 us
    pallas_call x2, Pallas kernels, attend(): pl.pallas_call(kernel, out_shape=out_shape, in_specs=[SMEM, SMEM] + [ANY...  10.4 us
    ppermute x12, waiting for transfers between devices, swap(): return lax.ppermute(array, 'ctx', [(i, i ^ flip) for i in range(4)])  7.25 us
    unnamed x16, local copies, waits for them, and re-layouts  4.16 us
    pallas_call x1, Pallas kernels, local(): pl.pallas_call(pack_slots, out_shape=[jax.ShapeDtypeStruct(shape, jnp.bfl...  1.05 us
  transfers between devices with their start and end apart: 12, of which 4 were waited for; matrix products, arithmetic and copies ran while one was open for 0% of the time, Pallas kernels for 18%

commit v1 on v0

--- a/solution.py
+++ b/solution.py
@@ -53,11 +53,7 @@
     return slice(head * HEAD_DIM, (head + 1) * HEAD_DIM)
 
 
-def needed(docs, me, block):
-    return (docs[block] >= docs[me * 4]) & (docs[block] <= docs[me * 4 + 3])
-
-
-def pack_slots(order, docs, *refs):
+def pack_slots(order, *refs):
     own, core, outs, held = refs[:3], refs[3:6], refs[6:9], refs[9:]
     me = lax.axis_index("ctx")
     for slot in range(3):
@@ -75,12 +71,9 @@
                 def _(sources=sources, rows=rows, head=head):
                     for array in range(3):
                         outs[1][1, array] = sources[array][rows, columns_of(head)]
-
-            @pl.when(needed(docs, me, block))
-            def _(sources=sources, rows=rows, block=block):
-                for array in range(3):
-                    for head in range(2):
-                        held[head][array, rows_of(block), :] = sources[array][rows, columns_of(head)]
+            for array in range(3):
+                for head in range(2):
+                    held[head][array, rows_of(block), :] = sources[array][rows, columns_of(head)]
 
 
 def one_doc(length, exact, start, end, base, blocks, keys_held, held, prob, dsc, results):
@@ -89,7 +82,7 @@
     whole = pl.ds(pl.multiple_of(window * BLOCK, BLOCK), rows)
     keys = keys_held[whole, :]
     values = held[0, whole, :]
-    pair = min(3 if exact and length != 4 else 2, length)
+    pair = min(3 if exact else 2, length)
     if not exact:
         key_block = window + lax.broadcasted_iota(jnp.int32, (rows, pair * BLOCK), 0) // BLOCK
         key_ok = (key_block >= start) & (key_block < end)
@@ -138,13 +131,19 @@
             )
         return
 
-    def fill(step, carry):
-        first = jnp.minimum(step * pair, length - pair)
-        columns = pl.ds(pl.multiple_of(first * BLOCK, BLOCK), pair * BLOCK)
+    def fill(first):
+        at = first * BLOCK
+        columns = pl.ds(at if exact else pl.multiple_of(at, BLOCK), pair * BLOCK)
         prob[0:rows, columns], dsc[0:rows, columns] = stats(first)
-        return carry
-
-    lax.fori_loop(0, -(-length // pair), fill, 0)
+
+    if exact:
+        for step in range(-(-length // pair)):
+            fill(min(step * pair, length - pair))
+    else:
+
+        @pl.loop(0, -(-length // pair))
+        def _(step):
+            fill(jnp.minimum(step * pair, length - pair))
     first = jnp.maximum(start, base)
     owned = jnp.minimum(end, base + 4) - first
     mine = pl.multiple_of((first - window) * BLOCK, BLOCK)
@@ -217,17 +216,12 @@
 
     for flip, source in enumerate(keys):
         for j in range(4):
-            block = order[(me ^ flip) * 4 + j]
-
-            @pl.when(needed(docs, me, block))
-            def _(source=source, j=j, block=block):
-                keys_held[rows_of(block), :] = source[j * BLOCK : (j + 1) * BLOCK, columns_of(head)]
-
-    def bring(block, source, at, also=True):
-        @pl.when(needed(docs, me, block) & also)
-        def _():
-            for array in range(3):
-                held[array, rows_of(block), :] = source[at, array]
+            to = rows_of(order[(me ^ flip) * 4 + j])
+            keys_held[to, :] = source[j * BLOCK : (j + 1) * BLOCK, columns_of(head)]
+
+    def bring(block, source, at):
+        for array in range(3):
+            held[array, rows_of(block), :] = source[at, array]
 
     for slot in range(3):
         for device, pieces in ((other, row), (other ^ 1, diag)):
@@ -238,7 +232,9 @@
     for position in range(1, 8):
         held_there |= order[other // 2 * 8 + position] == block
     for source, core_of in ((far_row, head), (far_diag, 1 - head)):
-        bring(block, source, source.shape[0] - 1, held_there & (me % 2 == core_of))
+        pl.when(held_there & (me % 2 == core_of))(
+            functools.partial(bring, block, source, source.shape[0] - 1)
+        )
 
     all_docs(blocks, longest, me * 4, docs, keys_held, held, prob, dsc, Results(head, outs, stage, sems))
 
@@ -334,11 +330,11 @@
     *packed, held0, held1 = pl.pallas_call(
         pack_slots,
         out_shape=[jax.ShapeDtypeStruct(shape, jnp.bfloat16) for shape in shapes],
-        in_specs=[SMEM] * 2 + [VMEM] * 6,
+        in_specs=[SMEM] + [VMEM] * 6,
         out_specs=[VMEM] * 5,
         compiler_params=pltpu.CompilerParams(vmem_limit_bytes=16 << 20),
         name="pack",
-    )(block_order, block_docs, *arrays[1:], *core[1:])
+    )(block_order, *arrays[1:], *core[1:])
     row = [swap(x, 2) for x in packed]
     all_keys = (keys, core[0], key_row, swap(key_row, 1))
     diag = [swap(x, 1) for x in row[:2]]

time: 34.9 us -> 33 us (0.946)
  the two profiles are of different devices: /device:TPU:1 before, /device:TPU:12 now
where the time goes in v1:
time: 33 us; the launch traced here: 32.6 us
  waiting for transfers between devices  13.3 us (40%)
  Pallas kernels  10.6 us (32%)
  starting transfers between devices  4.33 us (13%)
  local copies, waits for them, and re-layouts  3.52 us (11%)
  between operations  0.87 us (3%)
    ppermute x12, waiting for transfers between devices, swap(): return lax.ppermute(array, 'ctx', [(i, i ^ flip) for i in range(4)])  13.3 us
    pallas_call x2, Pallas kernels, attend(): pl.pallas_call(kernel, out_shape=out_shape, in_specs=[SMEM, SMEM] + [ANY...  9.53 us
    ppermute x12, starting transfers between devices, swap(): return lax.ppermute(array, 'ctx', [(i, i ^ flip) for i in range(4)])  4.33 us
    unnamed x14, local copies, waits for them, and re-layouts  3.52 us
    pallas_call x1, Pallas kernels, local(): pl.pallas_call(pack_slots, out_shape=[jax.ShapeDtypeStruct(shape, jnp.bfl...  1.06 us
  transfers between devices with their start and end apart: 12, of which 7 were waited for; matrix products, arithmetic and copies ran while one was open for 0% of the time, Pallas kernels for 18%

profile of v1, /device:TPU:12, one launch (start us, length us, event | category | flops | bytes accessed | tf_op | source)
XLA Modules:
  0.0 32.6 jit_solution(8917577819368120652)
XLA Ops:
  0.6 0.0 copy-start
  0.6 0.1 collective-permute-start.1
  0.7 0.5 %collective-permute-start = (bf16[512,256]{1,0:T(8,128)(2,1)}, bf16[512,256]{1,0:T(8,128)(2,1)S(1)}, u32[]{:S(2)}, u32[]{:S(2)}) collective-permute-start(bf16[512,256]{1,0:T(8,128)(2,1)} %refs_0_.1), channel_id=1, source_target_pairs={{0,4},{4,0},{8,12},{12,8},{1,5},{5,1},{9,13},{13,9},{2,6},{6,2},{1... | collective-permute-start | bytes 786440 | tf_op jit(solution)/shard_map/ppermute | solution.py:325
  1.2 0.1 collective-permute-start.2
  1.3 0.5 %collective-permute-start.4 = (bf16[512,256]{1,0:T(8,128)(2,1)}, bf16[512,256]{1,0:T(8,128)(2,1)S(1)}, u32[]{:S(2)}, u32[]{:S(2)}) collective-permute-start(bf16[512,256]{1,0:T(8,128)(2,1)} %refs_1_.5), channel_id=1, source_target_pairs={{0,8},{4,12},{8,0},{12,4},{1,9},{5,13},{9,1},{13,5},{2,10},{6,14},... | collective-permute-start | bytes 786440 | tf_op jit(solution)/shard_map/ppermute | solution.py:325
  1.8 0.7 %collective-permute-done.1.refs_4_ = bf16[512,256]{1,0:T(8,128)(2,1)S(1)} collective-permute-done((bf16[512,256]{1,0:T(8,128)(2,1)}, bf16[512,256]{1,0:T(8,128)(2,1)S(1)}, u32[]{:S(2)}, u32[]{:S(2)}) %collective-permute-start.1) | collective-permute-done | bytes 262176 | tf_op jit(solution)/shard_map/ppermute | solution.py:325
  2.5 0.4 %collective-permute-done.refs_3_ = bf16[512,256]{1,0:T(8,128)(2,1)S(1)} collective-permute-done((bf16[512,256]{1,0:T(8,128)(2,1)}, bf16[512,256]{1,0:T(8,128)(2,1)S(1)}, u32[]{:S(2)}, u32[]{:S(2)}) %collective-permute-start) | collective-permute-done | bytes 262176 | tf_op jit(solution)/shard_map/ppermute | solution.py:325
  2.8 0.4 %collective-permute-done.2.refs_5_ = bf16[512,256]{1,0:T(8,128)(2,1)S(1)} collective-permute-done((bf16[512,256]{1,0:T(8,128)(2,1)}, bf16[512,256]{1,0:T(8,128)(2,1)S(1)}, u32[]{:S(2)}, u32[]{:S(2)}) %collective-permute-start.2) | collective-permute-done | bytes 262176 | tf_op jit(solution)/shard_map/ppermute | solution.py:325
  3.2 0.0 copy-start.1
  3.2 0.9 %copy-done.1 = bf16[512,256]{1,0:T(8,128)(2,1)S(1)} copy-done((bf16[512,256]{1,0:T(8,128)(2,1)S(1)}, bf16[512,256]{1,0:T(8,128)(2,1)}, u32[]{:S(2)}) %copy-start.1) | copy-done | bytes 262168
  4.2 0.0 copy-start.2
  4.2 0.9 %copy-done.2 = bf16[512,256]{1,0:T(8,128)(2,1)S(1)} copy-done((bf16[512,256]{1,0:T(8,128)(2,1)S(1)}, bf16[512,256]{1,0:T(8,128)(2,1)}, u32[]{:S(2)}) %copy-start.2) | copy-done | bytes 262168
  5.1 0.0 copy-start.3
  5.1 0.9 %copy-done.3 = bf16[512,256]{1,0:T(8,128)(2,1)S(1)} copy-done((bf16[512,256]{1,0:T(8,128)(2,1)S(1)}, bf16[512,256]{1,0:T(8,128)(2,1)}, u32[]{:S(2)}) %copy-start.3) | copy-done | bytes 262168
  6.1 0.0 copy-start.4
  6.1 0.7 %copy-done.4 = s32[16]{0:T(128)S(1)} copy-done((s32[16]{0:T(128)S(1)}, s32[16]{0:T(128)}, u32[]{:S(2)}) %copy-start.4) | copy-done | bytes 88
  6.7 0.0 copy-start.5
  6.7 0.0 copy-start.6
  6.7 1.1 %pack.1 = (bf16[2,3,128,128]{3,2,1,0:T(8,128)(2,1)S(1)}, bf16[2,3,128,128]{3,2,1,0:T(8,128)(2,1)S(1)}, bf16[3,3,128,128]{3,2,1,0:T(8,128)(2,1)S(1)}, bf16[3,2048...) custom-call(s32[16]{0:T(128)S(1)} %copy-done.4, bf16[512,256]{1,0:T(8,128)(2,1)S(1)} %copy-done.1, ...), custom_call_target="tpu_custom_call" | custom-call | tf_op jit(solution)/shard_map/pack/pallas_call | solution.py:330
  7.8 0.6 %collective-permute-start.6 = (bf16[2,3,128,128]{3,2,1,0:T(8,128)(2,1)S(1)}, bf16[2,3,128,128]{3,2,1,0:T(8,128)(2,1)S(1)}, u32[]{:S(2)}, u32[]{:S(2)}) collective-permute-start(bf16[2,3,128,128]{3,2,1,0:T(8,128)(2,1)S(1)} %get-tuple-element.19), channel_id=1, source_target_pairs={{0,8},{4,12},{8,0},{12,4},{1,9},{5,13},{9,1},{13,5},{2,10},{6,14},... | collective-permute-start | bytes 589832 | tf_op jit(solution)/shard_map/ppermute | solution.py:325
  8.4 1.5 %collective-permute-start.9 = (bf16[2,3,128,128]{3,2,1,0:T(8,128)(2,1)S(1)}, bf16[2,3,128,128]{3,2,1,0:T(8,128)(2,1)S(1)}, u32[]{:S(2)}, u32[]{:S(2)}) collective-permute-start(bf16[2,3,128,128]{3,2,1,0:T(8,128)(2,1)S(1)} %get-tuple-element.22), channel_id=1, source_target_pairs={{0,8},{4,12},{8,0},{12,4},{1,9},{5,13},{9,1},{13,5},{2,10},{6,14},... | collective-permute-start | bytes 589832 | tf_op jit(solution)/shard_map/ppermute | solution.py:325
  9.9 0.5 %collective-permute-start.8 = (bf16[3,3,128,128]{3,2,1,0:T(8,128)(2,1)S(1)}, bf16[3,3,128,128]{3,2,1,0:T(8,128)(2,1)S(1)}, u32[]{:S(2)}, u32[]{:S(2)}) collective-permute-start(bf16[3,3,128,128]{3,2,1,0:T(8,128)(2,1)S(1)} %get-tuple-element.20), channel_id=1, source_target_pairs={{0,8},{4,12},{8,0},{12,4},{1,9},{5,13},{9,1},{13,5},{2,10},{6,14},... | collective-permute-start | bytes 884744 | tf_op jit(solution)/shard_map/ppermute | solution.py:325
  10.4 0.0 copy-done
  10.4 0.0 collective-permute-start.3
  10.4 0.0 collective-permute-done.4.refs_3_
  10.4 0.5 %collective-permute-start.5 = (bf16[512,256]{1,0:T(8,128)(2,1)S(1)}, bf16[512,256]{1,0:T(8,128)(2,1)S(1)}, u32[]{:S(2)}, u32[]{:S(2)}) collective-permute-start(bf16[512,256]{1,0:T(8,128)(2,1)S(1)} %collective-permute-done.4.refs_3_), channel_id=1, source_target_pairs={{0,4},{4,0},{8,12},{12,8},{1,5},{5,1},{9,13},{13,9},{2,6},{6,2},{1... | collective-permute-start | bytes 786440 | tf_op jit(solution)/shard_map/ppermute | solution.py:325
  10.9 4.7 %collective-permute-done.6.refs_5_.refs_8_ = bf16[2,3,128,128]{3,2,1,0:T(8,128)(2,1)S(1)} collective-permute-done((bf16[2,3,128,128]{3,2,1,0:T(8,128)(2,1)S(1)}, bf16[2,3,128,128]{3,2,1,0:T(8,128)(2,1)S(1)}, u32[]{:S(2)}, u32[]{:S(2)}) %collective-permute-start.6) | collective-permute-done | bytes 196640 | tf_op jit(solution)/shard_map/ppermute | solution.py:325
  15.6 0.0 collective-permute-start.7
  15.6 4.2 %collective-permute-done.9.refs_7_ = bf16[2,3,128,128]{3,2,1,0:T(8,128)(2,1)S(1)} collective-permute-done((bf16[2,3,128,128]{3,2,1,0:T(8,128)(2,1)S(1)}, bf16[2,3,128,128]{3,2,1,0:T(8,128)(2,1)S(1)}, u32[]{:S(2)}, u32[]{:S(2)}) %collective-permute-start.9) | collective-permute-done | bytes 196640 | tf_op jit(solution)/shard_map/ppermute | solution.py:325
  19.8 0.0 collective-permute-start.10
  19.8 0.0 collective-permute-done.3.refs_2_
  19.8 0.0 collective-permute-done.5.refs_4_
  19.8 0.0 collective-permute-done.7.refs_6_.refs_10_
  19.9 1.4 %collective-permute-done.10.refs_9_ = bf16[2,3,128,128]{3,2,1,0:T(8,128)(2,1)S(1)} collective-permute-done((bf16[2,3,128,128]{3,2,1,0:T(8,128)(2,1)S(1)}, bf16[2,3,128,128]{3,2,1,0:T(8,128)(2,1)S(1)}, u32[]{:S(2)}, u32[]{:S(2)}) %collective-permute-start.10) | collective-permute-done | bytes 196640 | tf_op jit(solution)/shard_map/ppermute | solution.py:325
  21.3 0.0 copy-done.5
  21.3 0.0 copy-done.6
  21.3 4.7 %attend.2 = (bf16[512,256]{1,0:T(8,128)(2,1)}, bf16[512,256]{1,0:T(8,128)(2,1)}, bf16[512,256]{1,0:T(8,128)(2,1)}, bf16[3,2048,128]{2,1,0:T(8,128)(2,1)S(1)}) custom-call(s32[16]{0:T(128)S(1)} %copy-done.5, s32[16]{0:T(128)S(1)} %copy-done.6, bf16[3,2048,128]{2,1,0:T(8,128)(2,1)S(1)} %get-tuple-element.21.refs_0_, ...), custom_call_target="tpu_custom_call", output_to_operand_aliasing={{3}: (2, {})} | custom-call | flops 1000000 | bytes 10000 | tf_op jit(solution)/shard_map/attend/pallas_call | solution.py:293
  26.0 0.0 collective-permute-done.8.refs_7_
  26.0 0.1 collective-permute-start.11
  26.1 1.6 %collective-permute-done.11.refs_8_ = bf16[3,3,128,128]{3,2,1,0:T(8,128)(2,1)S(1)} collective-permute-done((bf16[3,3,128,128]{3,2,1,0:T(8,128)(2,1)S(1)}, bf16[3,3,128,128]{3,2,1,0:T(8,128)(2,1)S(1)}, u32[]{:S(2)}, u32[]{:S(2)}) %collective-permute-start.11) | collective-permute-done | bytes 294944 | tf_op jit(solution)/shard_map/ppermute | solution.py:325
  27.6 4.9 %attend.3 = (bf16[512,256]{1,0:T(8,128)(2,1)}, bf16[512,256]{1,0:T(8,128)(2,1)}, bf16[512,256]{1,0:T(8,128)(2,1)}, bf16[3,2048,128]{2,1,0:T(8,128)(2,1)S(1)}) custom-call(s32[16]{0:T(128)S(1)} %copy-done.5, s32[16]{0:T(128)S(1)} %copy-done.6, ...), custom_call_target="tpu_custom_call", output_to_operand_aliasing={{0}: (11, {}), {1}: (12, {}), {2}: (13, {}), {3}: (2, {})} | custom-call | flops 1000000 | bytes 10000 | tf_op jit(solution)/shard_map/attend/pallas_call | solution.py:293
Async XLA Ops:
  0.6 9.8 %copy-start = (bf16[512,256]{1,0:T(8,128)(2,1)S(1)}, bf16[512,256]{1,0:T(8,128)(2,1)}, u32[]{:S(2)}) copy-start(bf16[512,256]{1,0:T(8,128)(2,1)} %refs_1_.5) | copy-start | bytes 786436
  0.6 1.8 %collective-permute-start.1 = (bf16[512,256]{1,0:T(8,128)(2,1)}, bf16[512,256]{1,0:T(8,128)(2,1)S(1)}, u32[]{:S(2)}, u32[]{:S(2)}) collective-permute-start(bf16[512,256]{1,0:T(8,128)(2,1)} %refs_1_.3), channel_id=1, source_target_pairs={{0,4},{4,0},{8,12},{12,8},{1,5},{5,1},{9,13},{13,9},{2,6},{6,2},{1... | collective-permute-start | bytes 786440 | tf_op jit(solution)/shard_map/ppermute | solution.py:325
  0.7 2.1 %collective-permute-start = (bf16[512,256]{1,0:T(8,128)(2,1)}, bf16[512,256]{1,0:T(8,128)(2,1)S(1)}, u32[]{:S(2)}, u32[]{:S(2)}) collective-permute-start(bf16[512,256]{1,0:T(8,128)(2,1)} %refs_0_.1), channel_id=1, source_target_pairs={{0,4},{4,0},{8,12},{12,8},{1,5},{5,1},{9,13},{13,9},{2,6},{6,2},{1... | collective-permute-start | bytes 786440 | tf_op jit(solution)/shard_map/ppermute | solution.py:325
  1.2 2.0 %collective-permute-start.2 = (bf16[512,256]{1,0:T(8,128)(2,1)}, bf16[512,256]{1,0:T(8,128)(2,1)S(1)}, u32[]{:S(2)}, u32[]{:S(2)}) collective-permute-start(bf16[512,256]{1,0:T(8,128)(2,1)} %refs_2_.1), channel_id=1, source_target_pairs={{0,4},{4,0},{8,12},{12,8},{1,5},{5,1},{9,13},{13,9},{2,6},{6,2},{1... | collective-permute-start | bytes 786440 | tf_op jit(solution)/shard_map/ppermute | solution.py:325
  1.3 9.1 %collective-permute-start.4 = (bf16[512,256]{1,0:T(8,128)(2,1)}, bf16[512,256]{1,0:T(8,128)(2,1)S(1)}, u32[]{:S(2)}, u32[]{:S(2)}) collective-permute-start(bf16[512,256]{1,0:T(8,128)(2,1)} %refs_1_.5), channel_id=1, source_target_pairs={{0,8},{4,12},{8,0},{12,4},{1,9},{5,13},{9,1},{13,5},{2,10},{6,14},... | collective-permute-start | bytes 786440 | tf_op jit(solution)/shard_map/ppermute | solution.py:325
  3.2 1.0 %copy-start.1 = (bf16[512,256]{1,0:T(8,128)(2,1)S(1)}, bf16[512,256]{1,0:T(8,128)(2,1)}, u32[]{:S(2)}) copy-start(bf16[512,256]{1,0:T(8,128)(2,1)} %refs_0_.1) | copy-start | bytes 786436
  4.2 0.9 %copy-start.2 = (bf16[512,256]{1,0:T(8,128)(2,1)S(1)}, bf16[512,256]{1,0:T(8,128)(2,1)}, u32[]{:S(2)}) copy-start(bf16[512,256]{1,0:T(8,128)(2,1)} %refs_1_.3) | copy-start | bytes 786436
  5.1 0.9 %copy-start.3 = (bf16[512,256]{1,0:T(8,128)(2,1)S(1)}, bf16[512,256]{1,0:T(8,128)(2,1)}, u32[]{:S(2)}) copy-start(bf16[512,256]{1,0:T(8,128)(2,1)} %refs_2_.1) | copy-start | bytes 786436
  6.1 0.7 %copy-start.4 = (s32[16]{0:T(128)S(1)}, s32[16]{0:T(128)}, u32[]{:S(2)}) copy-start(s32[16]{0:T(128)} %order.5) | copy-start | bytes 196
  6.7 14.6 %copy-start.5 = (s32[16]{0:T(128)S(1)}, s32[16]{0:T(128)}, u32[]{:S(2)}) copy-start(s32[16]{0:T(128)} %order.5) | copy-start | bytes 196
  6.7 14.6 %copy-start.6 = (s32[16]{0:T(128)S(1)}, s32[16]{0:T(128)}, u32[]{:S(2)}) copy-start(s32[16]{0:T(128)} %docs.3) | copy-start | bytes 196
  7.8 7.8 %collective-permute-start.6 = (bf16[2,3,128,128]{3,2,1,0:T(8,128)(2,1)S(1)}, bf16[2,3,128,128]{3,2,1,0:T(8,128)(2,1)S(1)}, u32[]{:S(2)}, u32[]{:S(2)}) collective-permute-start(bf16[2,3,128,128]{3,2,1,0:T(8,128)(2,1)S(1)} %get-tuple-element.19), channel_id=1, source_target_pairs={{0,8},{4,12},{8,0},{12,4},{1,9},{5,13},{9,1},{13,5},{2,10},{6,14},... | collective-permute-start | bytes 589832 | tf_op jit(solution)/shard_map/ppermute | solution.py:325
  8.4 11.5 %collective-permute-start.9 = (bf16[2,3,128,128]{3,2,1,0:T(8,128)(2,1)S(1)}, bf16[2,3,128,128]{3,2,1,0:T(8,128)(2,1)S(1)}, u32[]{:S(2)}, u32[]{:S(2)}) collective-permute-start(bf16[2,3,128,128]{3,2,1,0:T(8,128)(2,1)S(1)} %get-tuple-element.22), channel_id=1, source_target_pairs={{0,8},{4,12},{8,0},{12,4},{1,9},{5,13},{9,1},{13,5},{2,10},{6,14},... | collective-permute-start | bytes 589832 | tf_op jit(solution)/shard_map/ppermute | solution.py:325
  9.9 16.1 %collective-permute-start.8 = (bf16[3,3,128,128]{3,2,1,0:T(8,128)(2,1)S(1)}, bf16[3,3,128,128]{3,2,1,0:T(8,128)(2,1)S(1)}, u32[]{:S(2)}, u32[]{:S(2)}) collective-permute-start(bf16[3,3,128,128]{3,2,1,0:T(8,128)(2,1)S(1)} %get-tuple-element.20), channel_id=1, source_target_pairs={{0,8},{4,12},{8,0},{12,4},{1,9},{5,13},{9,1},{13,5},{2,10},{6,14},... | collective-permute-start | bytes 884744 | tf_op jit(solution)/shard_map/ppermute | solution.py:325
  10.4 9.4 %collective-permute-start.3 = (bf16[512,256]{1,0:T(8,128)(2,1)S(1)}, bf16[512,256]{1,0:T(8,128)(2,1)S(1)}, u32[]{:S(2)}, u32[]{:S(2)}) collective-permute-start(bf16[512,256]{1,0:T(8,128)(2,1)S(1)} %copy-done), channel_id=1, source_target_pairs={{0,4},{4,0},{8,12},{12,8},{1,5},{5,1},{9,13},{13,9},{2,6},{6,2},{1... | collective-permute-start | bytes 786440 | tf_op jit(solution)/shard_map/ppermute | solution.py:325
  10.4 9.4 %collective-permute-start.5 = (bf16[512,256]{1,0:T(8,128)(2,1)S(1)}, bf16[512,256]{1,0:T(8,128)(2,1)S(1)}, u32[]{:S(2)}, u32[]{:S(2)}) collective-permute-start(bf16[512,256]{1,0:T(8,128)(2,1)S(1)} %collective-permute-done.4.refs_3_), channel_id=1, source_target_pairs={{0,4},{4,0},{8,12},{12,8},{1,5},{5,1},{9,13},{13,9},{2,6},{6,2},{1... | collective-permute-start | bytes 786440 | tf_op jit(solution)/shard_map/ppermute | solution.py:325
  15.6 4.2 %collective-permute-start.7 = (bf16[2,3,128,128]{3,2,1,0:T(8,128)(2,1)S(1)}, bf16[2,3,128,128]{3,2,1,0:T(8,128)(2,1)S(1)}, u32[]{:S(2)}, u32[]{:S(2)}) collective-permute-start(bf16[2,3,128,128]{3,2,1,0:T(8,128)(2,1)S(1)} %collective-permute-done.6.refs_5_.refs_8_), channel_id=1, source_target_pairs={{0,4},{4,0},{8,12},{12,8},{1,5},{5,1},{9,13},{13,9},{2,6},{6,2},{1... | collective-permute-start | bytes 589832 | tf_op jit(solution)/shard_map/ppermute | solution.py:325
  19.8 1.4 %collective-permute-start.10 = (bf16[2,3,128,128]{3,2,1,0:T(8,128)(2,1)S(1)}, bf16[2,3,128,128]{3,2,1,0:T(8,128)(2,1)S(1)}, u32[]{:S(2)}, u32[]{:S(2)}) collective-permute-start(bf16[2,3,128,128]{3,2,1,0:T(8,128)(2,1)S(1)} %collective-permute-done.9.refs_7_), channel_id=1, source_target_pairs={{0,4},{4,0},{8,12},{12,8},{1,5},{5,1},{9,13},{13,9},{2,6},{6,2},{1... | collective-permute-start | bytes 589832 | tf_op jit(solution)/shard_map/ppermute | solution.py:325
  26.0 1.6 %collective-permute-start.11 = (bf16[3,3,128,128]{3,2,1,0:T(8,128)(2,1)S(1)}, bf16[3,3,128,128]{3,2,1,0:T(8,128)(2,1)S(1)}, u32[]{:S(2)}, u32[]{:S(2)}) collective-permute-start(bf16[3,3,128,128]{3,2,1,0:T(8,128)(2,1)S(1)} %collective-permute-done.8.refs_7_), channel_id=1, source_target_pairs={{0,4},{4,0},{8,12},{12,8},{1,5},{5,1},{9,13},{13,9},{2,6},{6,2},{1... | collective-permute-start | bytes 884744 | tf_op jit(solution)/shard_map/ppermute | solution.py:325

commit v2 on v1

--- a/solution.py
+++ b/solution.py
@@ -82,14 +82,14 @@
     whole = pl.ds(pl.multiple_of(window * BLOCK, BLOCK), rows)
     keys = keys_held[whole, :]
     values = held[0, whole, :]
-    pair = min(3 if exact else 2, length)
+    pair = min(2, length)
     if not exact:
         key_block = window + lax.broadcasted_iota(jnp.int32, (rows, pair * BLOCK), 0) // BLOCK
         key_ok = (key_block >= start) & (key_block < end)
 
-    def stats(first):
+    def stats(first, count):
         at = window + first
-        these = pl.ds(pl.multiple_of(at * BLOCK, BLOCK), pair * BLOCK)
+        these = pl.ds(pl.multiple_of(at * BLOCK, BLOCK), count * BLOCK)
         queries = held[1, these, :]
         douts = held[2, these, :]
         scores = dot(keys, queries, NT) * EXP2_SCALE
@@ -103,7 +103,7 @@
         delta = jnp.sum(probabilities * dprob, axis=0, keepdims=True)
         dscore = probabilities * (dprob - delta)
         if not exact:
-            query_block = at + lax.broadcasted_iota(jnp.int32, (rows, pair * BLOCK), 1) // BLOCK
+            query_block = at + lax.broadcasted_iota(jnp.int32, (rows, count * BLOCK), 1) // BLOCK
             ok = key_ok & (query_block >= start) & (query_block < end)
             probabilities = jnp.where(ok, probabilities, 0.0)
             dscore = jnp.where(ok, dscore, 0.0)
@@ -113,16 +113,13 @@
     douts = held[2, whole, :]
 
     def store(first, count, prob_rows, dsc_rows, dsc_columns):
-        def put(array, value):
-            results.stage[array, results.rows(first - base, count), :] = value.astype(jnp.bfloat16)
-            results.copy(array, first - base, count).start()
-
-        put(2, dot(prob_rows, douts, NN))
-        put(1, dot(dsc_rows, queries, NN) * SCALE)
-        put(0, dot(dsc_columns, keys, TN) * SCALE)
+        at = first - base
+        results.put(2, at, count, dot(prob_rows, douts, NN))
+        results.put(1, at, count, dot(dsc_rows, queries, NN) * SCALE)
+        results.put(0, at, count, dot(dsc_columns, keys, TN) * SCALE)
 
     if exact and length <= 2:
-        prob_low, dsc_low = stats(0)
+        prob_low, dsc_low = stats(0, length)
         for i in range(length):
             mine = slice(i * BLOCK, (i + 1) * BLOCK)
             block = start + i
@@ -131,19 +128,21 @@
             )
         return
 
-    def fill(first):
+    def fill(first, count):
         at = first * BLOCK
-        columns = pl.ds(at if exact else pl.multiple_of(at, BLOCK), pair * BLOCK)
-        prob[0:rows, columns], dsc[0:rows, columns] = stats(first)
+        columns = pl.ds(at if exact else pl.multiple_of(at, BLOCK), count * BLOCK)
+        prob[0:rows, columns], dsc[0:rows, columns] = stats(first, count)
 
     if exact:
-        for step in range(-(-length // pair)):
-            fill(min(step * pair, length - pair))
+        half = -(-length // 2)
+        fill(0, half)
+        fill(half, length - half)
     else:
 
         @pl.loop(0, -(-length // pair))
         def _(step):
-            fill(jnp.minimum(step * pair, length - pair))
+            fill(jnp.minimum(step * pair, length - pair), pair)
+
     first = jnp.maximum(start, base)
     owned = jnp.minimum(end, base + 4) - first
     mine = pl.multiple_of((first - window) * BLOCK, BLOCK)
@@ -161,6 +160,20 @@
 
     def rows(self, at, count):
         return pl.ds(pl.multiple_of(at * BLOCK, BLOCK), count * BLOCK)
+
+    def put(self, array, at, count, value):
+        self.stage[array, self.rows(at, count), :] = value.astype(jnp.bfloat16)
+        if self.outs:
+            self.copy(array, at, count).start()
+
+    def start(self):
+        for array in range(3):
+            self.copy(array, 0, 4).start()
+
+    def wait(self):
+        if self.outs:
+            for array in range(3):
+                self.copy(array, 0, 4).wait()
 
     def copy(self, array, at, count):
         rows = self.rows(at, count)
@@ -203,14 +216,21 @@
         return carry
 
     lax.fori_loop(0, 4, visit, 0)
-    for array in range(3):
-        results.copy(array, 0, 4).wait()
+    results.wait()
 
 
 def attend_slots(blocks, longest, head, order, docs, *refs):
     keys, (far_row, far_diag) = refs[1:5], refs[5:7]
-    row, diag = (refs[7:9], refs[9:11]) if head == 0 else (refs[7:8], refs[8:9])
-    outs, held, (prob, dsc, stage, sems, keys_held) = refs[-9:-6], refs[-6], refs[-5:]
+    if head == 0:
+        row, diag = refs[7:9], refs[9:11]
+        stage, held, prob, dsc, keys_held = refs[-5:]
+        results = Results(0, (), stage, None)
+    else:
+        row, diag, before = refs[7:8], refs[8:9], refs[9]
+        outs, (held, prob, dsc, keys_held, stage, sems) = refs[-9:-6], refs[-6:]
+        earlier = Results(0, outs, before, sems.at[pl.ds(3, 3)])
+        earlier.start()
+        results = Results(1, outs, stage, sems)
     me = lax.axis_index("ctx")
     other = me ^ 2
 
@@ -236,11 +256,13 @@
             functools.partial(bring, block, source, source.shape[0] - 1)
         )
 
-    all_docs(blocks, longest, me * 4, docs, keys_held, held, prob, dsc, Results(head, outs, stage, sems))
+    all_docs(blocks, longest, me * 4, docs, keys_held, held, prob, dsc, results)
+    if head:
+        earlier.wait()
 
 
 def attend_gathered(blocks, longest, head, order, docs, keys, values, queries, grad_out, *rest):
-    outs, (prob, dsc, stage, out_sems, keys_held, held, sems) = rest[-10:-7], rest[-7:]
+    outs, (prob, dsc, keys_held, stage, out_sems, held, sems) = rest[-10:-7], rest[-7:]
     me = lax.axis_index("ctx")
 
     def copies(position):
@@ -271,28 +293,29 @@
     all_docs(blocks, longest, me * 4, docs, keys_held, held, prob, dsc, results)
 
 
-def attend(kernel, sources, previous, order, docs, rows, blocks, longest, heads, gathered):
-    out_shape = [jax.ShapeDtypeStruct((rows, heads * HEAD_DIM), jnp.bfloat16)] * 3
-    out_specs = [ANY] * 3
+def attend(kernel, sources, previous, order, docs, rows, blocks, longest, heads, gathered, last=True):
+    staged = (3, 4 * BLOCK, HEAD_DIM)
     held = (ARRAYS - 1, blocks * BLOCK, HEAD_DIM)
+    shapes = [(rows, heads * HEAD_DIM)] * 3 if last else [staged]
+    out_specs = [ANY] * 3 if last else [VMEM]
     first = 2 + len(sources)
     aliases = {first + i: i for i in range(len(previous))}
     scratch = [
         pltpu.VMEM((longest * BLOCK, longest * BLOCK), jnp.bfloat16),
         pltpu.VMEM((longest * BLOCK, longest * BLOCK), jnp.bfloat16),
-        pltpu.VMEM((3, 4 * BLOCK, HEAD_DIM), jnp.bfloat16),
-        pltpu.SemaphoreType.DMA((3,)),
         pltpu.VMEM((blocks * BLOCK, HEAD_DIM), jnp.bfloat16),
     ]
+    if last:
+        scratch += [pltpu.VMEM(staged, jnp.bfloat16), pltpu.SemaphoreType.DMA((6,))]
     if gathered:
         scratch += [pltpu.VMEM(held, jnp.bfloat16), pltpu.SemaphoreType.DMA((blocks * ARRAYS,))]
     else:
-        out_shape.append(jax.ShapeDtypeStruct(held, jnp.bfloat16))
+        aliases[2] = len(shapes)
+        shapes.append(held)
         out_specs.append(VMEM)
-        aliases[2] = 3
     return pl.pallas_call(
         kernel,
-        out_shape=out_shape,
+        out_shape=[jax.ShapeDtypeStruct(shape, jnp.bfloat16) for shape in shapes],
         in_specs=[SMEM, SMEM] + [ANY if gathered else VMEM] * len(sources) + [ANY] * len(previous),
         out_specs=out_specs,
         scratch_shapes=scratch,
@@ -302,7 +325,7 @@
             flops=10**6, bytes_accessed=10**4, transcendentals=10**3
         ),
         name="attend",
-    )(order, docs, *sources, *previous)[:3]
+    )(order, docs, *sources, *previous)
 
 
 def local(queries, keys, values, grad_out, block_docs, block_order):
@@ -339,16 +362,17 @@
     all_keys = (keys, core[0], key_row, swap(key_row, 1))
     diag = [swap(x, 1) for x in row[:2]]
     far = (row[1], diag[1])
-    grads = attend(
+    sizes = (block_order, block_docs, rows, blocks, longest, heads, False)
+    before = attend(
         functools.partial(attend_slots, blocks, longest, 0),
-        (held0, *all_keys, *far, *row[:2], *diag), (), block_order, block_docs, rows, blocks, longest, heads, False,
-    )
-    last, grads = lax.optimization_barrier((row[2], grads))
+        (held0, *all_keys, *far, *row[:2], *diag), (), *sizes, last=False,
+    )[0]
+    last, before = lax.optimization_barrier((row[2], before))
     grads = attend(
         functools.partial(attend_slots, blocks, longest, 1),
-        (held1, *all_keys, *far, last, swap(last, 1)), grads, block_order, block_docs, rows, blocks, longest, heads, False,
+        (held1, *all_keys, *far, last, swap(last, 1), before), (), *sizes,
     )
-    return tuple(grads)
+    return tuple(grads[:3])
 
 
 def solution(mesh):

time: 33 us -> 32.8 us (level)
  transfers between devices with their start and end apart: 12 -> 12, of which waited for: 7 -> 7; matrix products, arithmetic and copies ran while one was open for 0% -> 0% of each run, Pallas kernels for 18% -> 16%
where the time goes in v2:
time: 32.8 us; the launch traced here: 32.4 us
  waiting for transfers between devices  13.3 us (41%)
  Pallas kernels  10.3 us (31%)
  starting transfers between devices  4.33 us (13%)
  local copies, waits for them, and re-layouts  3.52 us (11%)
  between operations  0.87 us (3%)
    ppermute x12, waiting for transfers between devices, swap(): return lax.ppermute(array, 'ctx', [(i, i ^ flip) for i in range(4)])  13.3 us
    pallas_call x2, Pallas kernels, attend(): pl.pallas_call(kernel, out_shape=[jax.ShapeDtypeStruct(shape, jnp.bfloat1...  9.26 us
    ppermute x12, starting transfers between devices, swap(): return lax.ppermute(array, 'ctx', [(i, i ^ flip) for i in range(4)])  4.33 us
    unnamed x14, local copies, waits for them, and re-layouts  3.52 us
    pallas_call x1, Pallas kernels, local(): pl.pallas_call(pack_slots, out_shape=[jax.ShapeDtypeStruct(shape, jnp.bfl...  1.08 us
  transfers between devices with their start and end apart: 12, of which 7 were waited for; matrix products, arithmetic and copies ran while one was open for 0% of the time, Pallas kernels for 16%

profile of v2, /device:TPU:12, one launch (start us, length us, event | category | flops | bytes accessed | tf_op | source)
XLA Modules:
  0.0 32.4 jit_solution(14905009839095229718)
XLA Ops:
  0.6 0.0 copy-start
  0.6 0.1 collective-permute-start.1
  0.7 0.5 %collective-permute-start = (bf16[512,256]{1,0:T(8,128)(2,1)}, bf16[512,256]{1,0:T(8,128)(2,1)S(1)}, u32[]{:S(2)}, u32[]{:S(2)}) collective-permute-start(bf16[512,256]{1,0:T(8,128)(2,1)} %refs_0_.1), channel_id=1, source_target_pairs={{0,4},{4,0},{8,12},{12,8},{1,5},{5,1},{9,13},{13,9},{2,6},{6,2},{1... | collective-permute-start | bytes 786440 | tf_op jit(solution)/shard_map/ppermute | solution.py:348
  1.2 0.1 collective-permute-start.2
  1.3 0.5 %collective-permute-start.4 = (bf16[512,256]{1,0:T(8,128)(2,1)}, bf16[512,256]{1,0:T(8,128)(2,1)S(1)}, u32[]{:S(2)}, u32[]{:S(2)}) collective-permute-start(bf16[512,256]{1,0:T(8,128)(2,1)} %refs_1_.5), channel_id=1, source_target_pairs={{0,8},{4,12},{8,0},{12,4},{1,9},{5,13},{9,1},{13,5},{2,10},{6,14},... | collective-permute-start | bytes 786440 | tf_op jit(solution)/shard_map/ppermute | solution.py:348
  1.8 0.7 %collective-permute-done.1.refs_4_ = bf16[512,256]{1,0:T(8,128)(2,1)S(1)} collective-permute-done((bf16[512,256]{1,0:T(8,128)(2,1)}, bf16[512,256]{1,0:T(8,128)(2,1)S(1)}, u32[]{:S(2)}, u32[]{:S(2)}) %collective-permute-start.1) | collective-permute-done | bytes 262176 | tf_op jit(solution)/shard_map/ppermute | solution.py:348
  2.5 0.4 %collective-permute-done.refs_3_ = bf16[512,256]{1,0:T(8,128)(2,1)S(1)} collective-permute-done((bf16[512,256]{1,0:T(8,128)(2,1)}, bf16[512,256]{1,0:T(8,128)(2,1)S(1)}, u32[]{:S(2)}, u32[]{:S(2)}) %collective-permute-start) | collective-permute-done | bytes 262176 | tf_op jit(solution)/shard_map/ppermute | solution.py:348
  2.8 0.4 %collective-permute-done.2.refs_5_ = bf16[512,256]{1,0:T(8,128)(2,1)S(1)} collective-permute-done((bf16[512,256]{1,0:T(8,128)(2,1)}, bf16[512,256]{1,0:T(8,128)(2,1)S(1)}, u32[]{:S(2)}, u32[]{:S(2)}) %collective-permute-start.2) | collective-permute-done | bytes 262176 | tf_op jit(solution)/shard_map/ppermute | solution.py:348
  3.2 0.0 copy-start.1
  3.2 0.9 %copy-done.1 = bf16[512,256]{1,0:T(8,128)(2,1)S(1)} copy-done((bf16[512,256]{1,0:T(8,128)(2,1)S(1)}, bf16[512,256]{1,0:T(8,128)(2,1)}, u32[]{:S(2)}) %copy-start.1) | copy-done | bytes 262168
  4.2 0.0 copy-start.2
  4.2 0.9 %copy-done.2 = bf16[512,256]{1,0:T(8,128)(2,1)S(1)} copy-done((bf16[512,256]{1,0:T(8,128)(2,1)S(1)}, bf16[512,256]{1,0:T(8,128)(2,1)}, u32[]{:S(2)}) %copy-start.2) | copy-done | bytes 262168
  5.1 0.0 copy-start.3
  5.1 0.9 %copy-done.3 = bf16[512,256]{1,0:T(8,128)(2,1)S(1)} copy-done((bf16[512,256]{1,0:T(8,128)(2,1)S(1)}, bf16[512,256]{1,0:T(8,128)(2,1)}, u32[]{:S(2)}) %copy-start.3) | copy-done | bytes 262168
  6.1 0.0 copy-start.4
  6.1 0.7 %copy-done.4 = s32[16]{0:T(128)S(1)} copy-done((s32[16]{0:T(128)S(1)}, s32[16]{0:T(128)}, u32[]{:S(2)}) %copy-start.4) | copy-done | bytes 88
  6.7 0.0 copy-start.5
  6.7 0.0 copy-start.6
  6.7 1.1 %pack.1 = (bf16[2,3,128,128]{3,2,1,0:T(8,128)(2,1)S(1)}, bf16[2,3,128,128]{3,2,1,0:T(8,128)(2,1)S(1)}, bf16[3,3,128,128]{3,2,1,0:T(8,128)(2,1)S(1)}, bf16[3,2048...) custom-call(s32[16]{0:T(128)S(1)} %copy-done.4, bf16[512,256]{1,0:T(8,128)(2,1)S(1)} %copy-done.1, ...), custom_call_target="tpu_custom_call" | custom-call | tf_op jit(solution)/shard_map/pack/pallas_call | solution.py:353
  7.8 0.6 %collective-permute-start.6 = (bf16[2,3,128,128]{3,2,1,0:T(8,128)(2,1)S(1)}, bf16[2,3,128,128]{3,2,1,0:T(8,128)(2,1)S(1)}, u32[]{:S(2)}, u32[]{:S(2)}) collective-permute-start(bf16[2,3,128,128]{3,2,1,0:T(8,128)(2,1)S(1)} %get-tuple-element.15), channel_id=1, source_target_pairs={{0,8},{4,12},{8,0},{12,4},{1,9},{5,13},{9,1},{13,5},{2,10},{6,14},... | collective-permute-start | bytes 589832 | tf_op jit(solution)/shard_map/ppermute | solution.py:348
  8.4 1.5 %collective-permute-start.9 = (bf16[2,3,128,128]{3,2,1,0:T(8,128)(2,1)S(1)}, bf16[2,3,128,128]{3,2,1,0:T(8,128)(2,1)S(1)}, u32[]{:S(2)}, u32[]{:S(2)}) collective-permute-start(bf16[2,3,128,128]{3,2,1,0:T(8,128)(2,1)S(1)} %get-tuple-element.18), channel_id=1, source_target_pairs={{0,8},{4,12},{8,0},{12,4},{1,9},{5,13},{9,1},{13,5},{2,10},{6,14},... | collective-permute-start | bytes 589832 | tf_op jit(solution)/shard_map/ppermute | solution.py:348
  9.9 0.5 %collective-permute-start.8 = (bf16[3,3,128,128]{3,2,1,0:T(8,128)(2,1)S(1)}, bf16[3,3,128,128]{3,2,1,0:T(8,128)(2,1)S(1)}, u32[]{:S(2)}, u32[]{:S(2)}) collective-permute-start(bf16[3,3,128,128]{3,2,1,0:T(8,128)(2,1)S(1)} %get-tuple-element.16), channel_id=1, source_target_pairs={{0,8},{4,12},{8,0},{12,4},{1,9},{5,13},{9,1},{13,5},{2,10},{6,14},... | collective-permute-start | bytes 884744 | tf_op jit(solution)/shard_map/ppermute | solution.py:348
  10.4 0.0 copy-done
  10.4 0.0 collective-permute-start.3
  10.4 0.0 collective-permute-done.4.refs_3_
  10.4 0.5 %collective-permute-start.5 = (bf16[512,256]{1,0:T(8,128)(2,1)S(1)}, bf16[512,256]{1,0:T(8,128)(2,1)S(1)}, u32[]{:S(2)}, u32[]{:S(2)}) collective-permute-start(bf16[512,256]{1,0:T(8,128)(2,1)S(1)} %collective-permute-done.4.refs_3_), channel_id=1, source_target_pairs={{0,4},{4,0},{8,12},{12,8},{1,5},{5,1},{9,13},{13,9},{2,6},{6,2},{1... | collective-permute-start | bytes 786440 | tf_op jit(solution)/shard_map/ppermute | solution.py:348
  10.9 4.7 %collective-permute-done.6.refs_5_.refs_8_ = bf16[2,3,128,128]{3,2,1,0:T(8,128)(2,1)S(1)} collective-permute-done((bf16[2,3,128,128]{3,2,1,0:T(8,128)(2,1)S(1)}, bf16[2,3,128,128]{3,2,1,0:T(8,128)(2,1)S(1)}, u32[]{:S(2)}, u32[]{:S(2)}) %collective-permute-start.6) | collective-permute-done | bytes 196640 | tf_op jit(solution)/shard_map/ppermute | solution.py:348
  15.6 0.0 collective-permute-start.7
  15.6 4.2 %collective-permute-done.9.refs_7_ = bf16[2,3,128,128]{3,2,1,0:T(8,128)(2,1)S(1)} collective-permute-done((bf16[2,3,128,128]{3,2,1,0:T(8,128)(2,1)S(1)}, bf16[2,3,128,128]{3,2,1,0:T(8,128)(2,1)S(1)}, u32[]{:S(2)}, u32[]{:S(2)}) %collective-permute-start.9) | collective-permute-done | bytes 196640 | tf_op jit(solution)/shard_map/ppermute | solution.py:348
  19.8 0.0 collective-permute-start.10
  19.9 0.0 collective-permute-done.3.refs_2_
  19.9 0.0 collective-permute-done.5.refs_4_
  19.9 0.0 collective-permute-done.7.refs_6_.refs_10_
  19.9 1.4 %collective-permute-done.10.refs_9_ = bf16[2,3,128,128]{3,2,1,0:T(8,128)(2,1)S(1)} collective-permute-done((bf16[2,3,128,128]{3,2,1,0:T(8,128)(2,1)S(1)}, bf16[2,3,128,128]{3,2,1,0:T(8,128)(2,1)S(1)}, u32[]{:S(2)}, u32[]{:S(2)}) %collective-permute-start.10) | collective-permute-done | bytes 196640 | tf_op jit(solution)/shard_map/ppermute | solution.py:348
  21.3 0.0 copy-done.5
  21.3 0.0 copy-done.6
  21.3 4.2 %attend.2 = (bf16[3,512,128]{2,1,0:T(8,128)(2,1)S(1)}, bf16[3,2048,128]{2,1,0:T(8,128)(2,1)S(1)}) custom-call(s32[16]{0:T(128)S(1)} %copy-done.5, s32[16]{0:T(128)S(1)} %copy-done.6, bf16[3,2048,128]{2,1,0:T(8,128)(2,1)S(1)} %get-tuple-element.17.refs_0_, bf16[512,256]{1,0:T(8,128)(2,1)S(1)} %copy-done, ...), custom_call_target="tpu_custom_call", output_to_operand_aliasing={{1}: (2, {})} | custom-call | flops 1000000 | bytes 10000 | tf_op jit(solution)/shard_map/attend/pallas_call | solution.py:316
  25.5 0.0 collective-permute-done.8.refs_7_
  25.5 0.1 collective-permute-start.11
  25.6 1.6 %collective-permute-done.11.refs_8_ = bf16[3,3,128,128]{3,2,1,0:T(8,128)(2,1)S(1)} collective-permute-done((bf16[3,3,128,128]{3,2,1,0:T(8,128)(2,1)S(1)}, bf16[3,3,128,128]{3,2,1,0:T(8,128)(2,1)S(1)}, u32[]{:S(2)}, u32[]{:S(2)}) %collective-permute-start.11) | collective-permute-done | bytes 294944 | tf_op jit(solution)/shard_map/ppermute | solution.py:348
  27.2 5.1 %attend.3 = (bf16[512,256]{1,0:T(8,128)(2,1)}, bf16[512,256]{1,0:T(8,128)(2,1)}, bf16[512,256]{1,0:T(8,128)(2,1)}, bf16[3,2048,128]{2,1,0:T(8,128)(2,1)S(1)}) custom-call(s32[16]{0:T(128)S(1)} %copy-done.5, s32[16]{0:T(128)S(1)} %copy-done.6, bf16[3,2048,128]{2,1,0:T(8,128)(2,1)S(1)} %get-tuple-element.14.refs_0_, ...), custom_call_target="tpu_custom_call", output_to_operand_aliasing={{3}: (2, {})} | custom-call | flops 1000000 | bytes 10000 | tf_op jit(solution)/shard_map/attend/pallas_call | solution.py:316
Async XLA Ops:
  0.6 9.8 %copy-start = (bf16[512,256]{1,0:T(8,128)(2,1)S(1)}, bf16[512,256]{1,0:T(8,128)(2,1)}, u32[]{:S(2)}) copy-start(bf16[512,256]{1,0:T(8,128)(2,1)} %refs_1_.5) | copy-start | bytes 786436
  0.6 1.8 %collective-permute-start.1 = (bf16[512,256]{1,0:T(8,128)(2,1)}, bf16[512,256]{1,0:T(8,128)(2,1)S(1)}, u32[]{:S(2)}, u32[]{:S(2)}) collective-permute-start(bf16[512,256]{1,0:T(8,128)(2,1)} %refs_1_.3), channel_id=1, source_target_pairs={{0,4},{4,0},{8,12},{12,8},{1,5},{5,1},{9,13},{13,9},{2,6},{6,2},{1... | collective-permute-start | bytes 786440 | tf_op jit(solution)/shard_map/ppermute | solution.py:348
  0.7 2.1 %collective-permute-start = (bf16[512,256]{1,0:T(8,128)(2,1)}, bf16[512,256]{1,0:T(8,128)(2,1)S(1)}, u32[]{:S(2)}, u32[]{:S(2)}) collective-permute-start(bf16[512,256]{1,0:T(8,128)(2,1)} %refs_0_.1), channel_id=1, source_target_pairs={{0,4},{4,0},{8,12},{12,8},{1,5},{5,1},{9,13},{13,9},{2,6},{6,2},{1... | collective-permute-start | bytes 786440 | tf_op jit(solution)/shard_map/ppermute | solution.py:348
  1.2 2.0 %collective-permute-start.2 = (bf16[512,256]{1,0:T(8,128)(2,1)}, bf16[512,256]{1,0:T(8,128)(2,1)S(1)}, u32[]{:S(2)}, u32[]{:S(2)}) collective-permute-start(bf16[512,256]{1,0:T(8,128)(2,1)} %refs_2_.1), channel_id=1, source_target_pairs={{0,4},{4,0},{8,12},{12,8},{1,5},{5,1},{9,13},{13,9},{2,6},{6,2},{1... | collective-permute-start | bytes 786440 | tf_op jit(solution)/shard_map/ppermute | solution.py:348
  1.3 9.1 %collective-permute-start.4 = (bf16[512,256]{1,0:T(8,128)(2,1)}, bf16[512,256]{1,0:T(8,128)(2,1)S(1)}, u32[]{:S(2)}, u32[]{:S(2)}) collective-permute-start(bf16[512,256]{1,0:T(8,128)(2,1)} %refs_1_.5), channel_id=1, source_target_pairs={{0,8},{4,12},{8,0},{12,4},{1,9},{5,13},{9,1},{13,5},{2,10},{6,14},... | collective-permute-start | bytes 786440 | tf_op jit(solution)/shard_map/ppermute | solution.py:348
  3.2 1.0 %copy-start.1 = (bf16[512,256]{1,0:T(8,128)(2,1)S(1)}, bf16[512,256]{1,0:T(8,128)(2,1)}, u32[]{:S(2)}) copy-start(bf16[512,256]{1,0:T(8,128)(2,1)} %refs_0_.1) | copy-start | bytes 786436
  4.2 0.9 %copy-start.2 = (bf16[512,256]{1,0:T(8,128)(2,1)S(1)}, bf16[512,256]{1,0:T(8,128)(2,1)}, u32[]{:S(2)}) copy-start(bf16[512,256]{1,0:T(8,128)(2,1)} %refs_1_.3) | copy-start | bytes 786436
  5.1 0.9 %copy-start.3 = (bf16[512,256]{1,0:T(8,128)(2,1)S(1)}, bf16[512,256]{1,0:T(8,128)(2,1)}, u32[]{:S(2)}) copy-start(bf16[512,256]{1,0:T(8,128)(2,1)} %refs_2_.1) | copy-start | bytes 786436
  6.1 0.7 %copy-start.4 = (s32[16]{0:T(128)S(1)}, s32[16]{0:T(128)}, u32[]{:S(2)}) copy-start(s32[16]{0:T(128)} %order.5) | copy-start | bytes 196
  6.7 14.6 %copy-start.5 = (s32[16]{0:T(128)S(1)}, s32[16]{0:T(128)}, u32[]{:S(2)}) copy-start(s32[16]{0:T(128)} %order.5) | copy-start | bytes 196
  6.7 14.6 %copy-start.6 = (s32[16]{0:T(128)S(1)}, s32[16]{0:T(128)}, u32[]{:S(2)}) copy-start(s32[16]{0:T(128)} %docs.3) | copy-start | bytes 196
  7.8 7.8 %collective-permute-start.6 = (bf16[2,3,128,128]{3,2,1,0:T(8,128)(2,1)S(1)}, bf16[2,3,128,128]{3,2,1,0:T(8,128)(2,1)S(1)}, u32[]{:S(2)}, u32[]{:S(2)}) collective-permute-start(bf16[2,3,128,128]{3,2,1,0:T(8,128)(2,1)S(1)} %get-tuple-element.15), channel_id=1, source_target_pairs={{0,8},{4,12},{8,0},{12,4},{1,9},{5,13},{9,1},{13,5},{2,10},{6,14},... | collective-permute-start | bytes 589832 | tf_op jit(solution)/shard_map/ppermute | solution.py:348
  8.4 11.5 %collective-permute-start.9 = (bf16[2,3,128,128]{3,2,1,0:T(8,128)(2,1)S(1)}, bf16[2,3,128,128]{3,2,1,0:T(8,128)(2,1)S(1)}, u32[]{:S(2)}, u32[]{:S(2)}) collective-permute-start(bf16[2,3,128,128]{3,2,1,0:T(8,128)(2,1)S(1)} %get-tuple-element.18), channel_id=1, source_target_pairs={{0,8},{4,12},{8,0},{12,4},{1,9},{5,13},{9,1},{13,5},{2,10},{6,14},... | collective-permute-start | bytes 589832 | tf_op jit(solution)/shard_map/ppermute | solution.py:348
  9.9 15.6 %collective-permute-start.8 = (bf16[3,3,128,128]{3,2,1,0:T(8,128)(2,1)S(1)}, bf16[3,3,128,128]{3,2,1,0:T(8,128)(2,1)S(1)}, u32[]{:S(2)}, u32[]{:S(2)}) collective-permute-start(bf16[3,3,128,128]{3,2,1,0:T(8,128)(2,1)S(1)} %get-tuple-element.16), channel_id=1, source_target_pairs={{0,8},{4,12},{8,0},{12,4},{1,9},{5,13},{9,1},{13,5},{2,10},{6,14},... | collective-permute-start | bytes 884744 | tf_op jit(solution)/shard_map/ppermute | solution.py:348
  10.4 9.5 %collective-permute-start.3 = (bf16[512,256]{1,0:T(8,128)(2,1)S(1)}, bf16[512,256]{1,0:T(8,128)(2,1)S(1)}, u32[]{:S(2)}, u32[]{:S(2)}) collective-permute-start(bf16[512,256]{1,0:T(8,128)(2,1)S(1)} %copy-done), channel_id=1, source_target_pairs={{0,4},{4,0},{8,12},{12,8},{1,5},{5,1},{9,13},{13,9},{2,6},{6,2},{1... | collective-permute-start | bytes 786440 | tf_op jit(solution)/shard_map/ppermute | solution.py:348
  10.4 9.4 %collective-permute-start.5 = (bf16[512,256]{1,0:T(8,128)(2,1)S(1)}, bf16[512,256]{1,0:T(8,128)(2,1)S(1)}, u32[]{:S(2)}, u32[]{:S(2)}) collective-permute-start(bf16[512,256]{1,0:T(8,128)(2,1)S(1)} %collective-permute-done.4.refs_3_), channel_id=1, source_target_pairs={{0,4},{4,0},{8,12},{12,8},{1,5},{5,1},{9,13},{13,9},{2,6},{6,2},{1... | collective-permute-start | bytes 786440 | tf_op jit(solution)/shard_map/ppermute | solution.py:348
  15.6 4.2 %collective-permute-start.7 = (bf16[2,3,128,128]{3,2,1,0:T(8,128)(2,1)S(1)}, bf16[2,3,128,128]{3,2,1,0:T(8,128)(2,1)S(1)}, u32[]{:S(2)}, u32[]{:S(2)}) collective-permute-start(bf16[2,3,128,128]{3,2,1,0:T(8,128)(2,1)S(1)} %collective-permute-done.6.refs_5_.refs_8_), channel_id=1, source_target_pairs={{0,4},{4,0},{8,12},{12,8},{1,5},{5,1},{9,13},{13,9},{2,6},{6,2},{1... | collective-permute-start | bytes 589832 | tf_op jit(solution)/shard_map/ppermute | solution.py:348
  19.8 1.4 %collective-permute-start.10 = (bf16[2,3,128,128]{3,2,1,0:T(8,128)(2,1)S(1)}, bf16[2,3,128,128]{3,2,1,0:T(8,128)(2,1)S(1)}, u32[]{:S(2)}, u32[]{:S(2)}) collective-permute-start(bf16[2,3,128,128]{3,2,1,0:T(8,128)(2,1)S(1)} %collective-permute-done.9.refs_7_), channel_id=1, source_target_pairs={{0,4},{4,0},{8,12},{12,8},{1,5},{5,1},{9,13},{13,9},{2,6},{6,2},{1... | collective-permute-start | bytes 589832 | tf_op jit(solution)/shard_map/ppermute | solution.py:348
  25.5 1.6 %collective-permute-start.11 = (bf16[3,3,128,128]{3,2,1,0:T(8,128)(2,1)S(1)}, bf16[3,3,128,128]{3,2,1,0:T(8,128)(2,1)S(1)}, u32[]{:S(2)}, u32[]{:S(2)}) collective-permute-start(bf16[3,3,128,128]{3,2,1,0:T(8,128)(2,1)S(1)} %collective-permute-done.8.refs_7_), channel_id=1, source_target_pairs={{0,4},{4,0},{8,12},{12,8},{1,5},{5,1},{9,13},{13,9},{2,6},{6,2},{1... | collective-permute-start | bytes 884744 | tf_op jit(solution)/shard_map/ppermute | solution.py:348

commit v3 on v2

--- a/solution.py
+++ b/solution.py
@@ -116,7 +116,11 @@
         at = first - base
         results.put(2, at, count, dot(prob_rows, douts, NN))
         results.put(1, at, count, dot(dsc_rows, queries, NN) * SCALE)
-        results.put(0, at, count, dot(dsc_columns, keys, TN) * SCALE)
+        half = -(-count // 2)
+        for lo, hi in ((0, half), (half, count)):
+            if hi > lo:
+                part = dsc_columns[:, lo * BLOCK : hi * BLOCK]
+                results.put(0, at + lo, hi - lo, dot(part, keys, TN) * SCALE)
 
     if exact and length <= 2:
         prob_low, dsc_low = stats(0, length)

time: 32.8 us -> 33.1 us (level); the launches traced: 32.4 us -> 33.3 us
  Pallas kernels: 10.3 us -> 11.3 us
    pallas_call x2, Pallas kernels: 9.26 us -> 10.2 us  [attend(): pl.pallas_call(kernel, out_shape=[jax.ShapeDtypeStruct(shape, jnp.bfloat1...]
  transfers between devices with their start and end apart: 12 -> 12, of which waited for: 7 -> 7; matrix products, arithmetic and copies ran while one was open for 0% -> 0% of each run, Pallas kernels for 16% -> 17%
where the time goes in v3:
time: 33.1 us; the launch traced here: 33.3 us
  waiting for transfers between devices  13.3 us (40%)
  Pallas kernels  11.3 us (34%)
  starting transfers between devices  4.35 us (13%)
  local copies, waits for them, and re-layouts  3.52 us (11%)
  between operations  0.87 us (3%)
    ppermute x12, waiting for transfers between devices, swap(): return lax.ppermute(array, 'ctx', [(i, i ^ flip) for i in range(4)])  13.3 us
    pallas_call x2, Pallas kernels, attend(): pl.pallas_call(kernel, out_shape=[jax.ShapeDtypeStruct(shape, jnp.bfloat1...  10.2 us
    ppermute x12, starting transfers between devices, swap(): return lax.ppermute(array, 'ctx', [(i, i ^ flip) for i in range(4)])  4.35 us
    unnamed x14, local copies, waits for them, and re-layouts  3.52 us
    pallas_call x1, Pallas kernels, local(): pl.pallas_call(pack_slots, out_shape=[jax.ShapeDtypeStruct(shape, jnp.bfl...  1.06 us
  transfers between devices with their start and end apart: 12, of which 7 were waited for; matrix products, arithmetic and copies ran while one was open for 0% of the time, Pallas kernels for 17%

profile of v3, /device:TPU:12, one launch (start us, length us, event | category | flops | bytes accessed | tf_op | source)
XLA Modules:
  0.0 33.3 jit_solution(294807486312377207)
XLA Ops:
  0.6 0.0 copy-start
  0.6 0.1 collective-permute-start.1
  0.7 0.5 %collective-permute-start = (bf16[512,256]{1,0:T(8,128)(2,1)}, bf16[512,256]{1,0:T(8,128)(2,1)S(1)}, u32[]{:S(2)}, u32[]{:S(2)}) collective-permute-start(bf16[512,256]{1,0:T(8,128)(2,1)} %refs_0_.1), channel_id=1, source_target_pairs={{0,4},{4,0},{8,12},{12,8},{1,5},{5,1},{9,13},{13,9},{2,6},{6,2},{1... | collective-permute-start | bytes 786440 | tf_op jit(solution)/shard_map/ppermute | solution.py:352
  1.2 0.1 collective-permute-start.2
  1.3 0.5 %collective-permute-start.4 = (bf16[512,256]{1,0:T(8,128)(2,1)}, bf16[512,256]{1,0:T(8,128)(2,1)S(1)}, u32[]{:S(2)}, u32[]{:S(2)}) collective-permute-start(bf16[512,256]{1,0:T(8,128)(2,1)} %refs_1_.5), channel_id=1, source_target_pairs={{0,8},{4,12},{8,0},{12,4},{1,9},{5,13},{9,1},{13,5},{2,10},{6,14},... | collective-permute-start | bytes 786440 | tf_op jit(solution)/shard_map/ppermute | solution.py:352
  1.8 0.7 %collective-permute-done.1.refs_4_ = bf16[512,256]{1,0:T(8,128)(2,1)S(1)} collective-permute-done((bf16[512,256]{1,0:T(8,128)(2,1)}, bf16[512,256]{1,0:T(8,128)(2,1)S(1)}, u32[]{:S(2)}, u32[]{:S(2)}) %collective-permute-start.1) | collective-permute-done | bytes 262176 | tf_op jit(solution)/shard_map/ppermute | solution.py:352
  2.5 0.4 %collective-permute-done.refs_3_ = bf16[512,256]{1,0:T(8,128)(2,1)S(1)} collective-permute-done((bf16[512,256]{1,0:T(8,128)(2,1)}, bf16[512,256]{1,0:T(8,128)(2,1)S(1)}, u32[]{:S(2)}, u32[]{:S(2)}) %collective-permute-start) | collective-permute-done | bytes 262176 | tf_op jit(solution)/shard_map/ppermute | solution.py:352
  2.8 0.4 %collective-permute-done.2.refs_5_ = bf16[512,256]{1,0:T(8,128)(2,1)S(1)} collective-permute-done((bf16[512,256]{1,0:T(8,128)(2,1)}, bf16[512,256]{1,0:T(8,128)(2,1)S(1)}, u32[]{:S(2)}, u32[]{:S(2)}) %collective-permute-start.2) | collective-permute-done | bytes 262176 | tf_op jit(solution)/shard_map/ppermute | solution.py:352
  3.2 0.0 copy-start.1
  3.2 0.9 %copy-done.1 = bf16[512,256]{1,0:T(8,128)(2,1)S(1)} copy-done((bf16[512,256]{1,0:T(8,128)(2,1)S(1)}, bf16[512,256]{1,0:T(8,128)(2,1)}, u32[]{:S(2)}) %copy-start.1) | copy-done | bytes 262168
  4.2 0.0 copy-start.2
  4.2 0.9 %copy-done.2 = bf16[512,256]{1,0:T(8,128)(2,1)S(1)} copy-done((bf16[512,256]{1,0:T(8,128)(2,1)S(1)}, bf16[512,256]{1,0:T(8,128)(2,1)}, u32[]{:S(2)}) %copy-start.2) | copy-done | bytes 262168
  5.1 0.0 copy-start.3
  5.1 0.9 %copy-done.3 = bf16[512,256]{1,0:T(8,128)(2,1)S(1)} copy-done((bf16[512,256]{1,0:T(8,128)(2,1)S(1)}, bf16[512,256]{1,0:T(8,128)(2,1)}, u32[]{:S(2)}) %copy-start.3) | copy-done | bytes 262168
  6.1 0.0 copy-start.4
  6.1 0.7 %copy-done.4 = s32[16]{0:T(128)S(1)} copy-done((s32[16]{0:T(128)S(1)}, s32[16]{0:T(128)}, u32[]{:S(2)}) %copy-start.4) | copy-done | bytes 88
  6.7 0.0 copy-start.5
  6.7 0.0 copy-start.6
  6.7 1.1 %pack.1 = (bf16[2,3,128,128]{3,2,1,0:T(8,128)(2,1)S(1)}, bf16[2,3,128,128]{3,2,1,0:T(8,128)(2,1)S(1)}, bf16[3,3,128,128]{3,2,1,0:T(8,128)(2,1)S(1)}, bf16[3,2048...) custom-call(s32[16]{0:T(128)S(1)} %copy-done.4, bf16[512,256]{1,0:T(8,128)(2,1)S(1)} %copy-done.1, ...), custom_call_target="tpu_custom_call" | custom-call | tf_op jit(solution)/shard_map/pack/pallas_call | solution.py:357
  7.8 0.6 %collective-permute-start.6 = (bf16[2,3,128,128]{3,2,1,0:T(8,128)(2,1)S(1)}, bf16[2,3,128,128]{3,2,1,0:T(8,128)(2,1)S(1)}, u32[]{:S(2)}, u32[]{:S(2)}) collective-permute-start(bf16[2,3,128,128]{3,2,1,0:T(8,128)(2,1)S(1)} %get-tuple-element.15), channel_id=1, source_target_pairs={{0,8},{4,12},{8,0},{12,4},{1,9},{5,13},{9,1},{13,5},{2,10},{6,14},... | collective-permute-start | bytes 589832 | tf_op jit(solution)/shard_map/ppermute | solution.py:352
  8.4 1.5 %collective-permute-start.9 = (bf16[2,3,128,128]{3,2,1,0:T(8,128)(2,1)S(1)}, bf16[2,3,128,128]{3,2,1,0:T(8,128)(2,1)S(1)}, u32[]{:S(2)}, u32[]{:S(2)}) collective-permute-start(bf16[2,3,128,128]{3,2,1,0:T(8,128)(2,1)S(1)} %get-tuple-element.18), channel_id=1, source_target_pairs={{0,8},{4,12},{8,0},{12,4},{1,9},{5,13},{9,1},{13,5},{2,10},{6,14},... | collective-permute-start | bytes 589832 | tf_op jit(solution)/shard_map/ppermute | solution.py:352
  9.9 0.5 %collective-permute-start.8 = (bf16[3,3,128,128]{3,2,1,0:T(8,128)(2,1)S(1)}, bf16[3,3,128,128]{3,2,1,0:T(8,128)(2,1)S(1)}, u32[]{:S(2)}, u32[]{:S(2)}) collective-permute-start(bf16[3,3,128,128]{3,2,1,0:T(8,128)(2,1)S(1)} %get-tuple-element.16), channel_id=1, source_target_pairs={{0,8},{4,12},{8,0},{12,4},{1,9},{5,13},{9,1},{13,5},{2,10},{6,14},... | collective-permute-start | bytes 884744 | tf_op jit(solution)/shard_map/ppermute | solution.py:352
  10.4 0.0 copy-done
  10.4 0.0 collective-permute-start.3
  10.4 0.0 collective-permute-done.4.refs_3_
  10.4 0.5 %collective-permute-start.5 = (bf16[512,256]{1,0:T(8,128)(2,1)S(1)}, bf16[512,256]{1,0:T(8,128)(2,1)S(1)}, u32[]{:S(2)}, u32[]{:S(2)}) collective-permute-start(bf16[512,256]{1,0:T(8,128)(2,1)S(1)} %collective-permute-done.4.refs_3_), channel_id=1, source_target_pairs={{0,4},{4,0},{8,12},{12,8},{1,5},{5,1},{9,13},{13,9},{2,6},{6,2},{1... | collective-permute-start | bytes 786440 | tf_op jit(solution)/shard_map/ppermute | solution.py:352
  10.9 4.7 %collective-permute-done.6.refs_5_.refs_8_ = bf16[2,3,128,128]{3,2,1,0:T(8,128)(2,1)S(1)} collective-permute-done((bf16[2,3,128,128]{3,2,1,0:T(8,128)(2,1)S(1)}, bf16[2,3,128,128]{3,2,1,0:T(8,128)(2,1)S(1)}, u32[]{:S(2)}, u32[]{:S(2)}) %collective-permute-start.6) | collective-permute-done | bytes 196640 | tf_op jit(solution)/shard_map/ppermute | solution.py:352
  15.6 0.0 collective-permute-start.7
  15.6 4.2 %collective-permute-done.9.refs_7_ = bf16[2,3,128,128]{3,2,1,0:T(8,128)(2,1)S(1)} collective-permute-done((bf16[2,3,128,128]{3,2,1,0:T(8,128)(2,1)S(1)}, bf16[2,3,128,128]{3,2,1,0:T(8,128)(2,1)S(1)}, u32[]{:S(2)}, u32[]{:S(2)}) %collective-permute-start.9) | collective-permute-done | bytes 196640 | tf_op jit(solution)/shard_map/ppermute | solution.py:352
  19.8 0.0 collective-permute-start.10
  19.8 0.0 collective-permute-done.3.refs_2_
  19.8 0.0 collective-permute-done.5.refs_4_
  19.8 0.0 collective-permute-done.7.refs_6_.refs_10_
  19.9 1.4 %collective-permute-done.10.refs_9_ = bf16[2,3,128,128]{3,2,1,0:T(8,128)(2,1)S(1)} collective-permute-done((bf16[2,3,128,128]{3,2,1,0:T(8,128)(2,1)S(1)}, bf16[2,3,128,128]{3,2,1,0:T(8,128)(2,1)S(1)}, u32[]{:S(2)}, u32[]{:S(2)}) %collective-permute-start.10) | collective-permute-done | bytes 196640 | tf_op jit(solution)/shard_map/ppermute | solution.py:352
  21.3 0.0 copy-done.5
  21.3 0.0 copy-done.6
  21.3 4.7 %attend.2 = (bf16[3,512,128]{2,1,0:T(8,128)(2,1)S(1)}, bf16[3,2048,128]{2,1,0:T(8,128)(2,1)S(1)}) custom-call(s32[16]{0:T(128)S(1)} %copy-done.5, s32[16]{0:T(128)S(1)} %copy-done.6, bf16[3,2048,128]{2,1,0:T(8,128)(2,1)S(1)} %get-tuple-element.17.refs_0_, bf16[512,256]{1,0:T(8,128)(2,1)S(1)} %copy-done, ...), custom_call_target="tpu_custom_call", output_to_operand_aliasing={{1}: (2, {})} | custom-call | flops 1000000 | bytes 10000 | tf_op jit(solution)/shard_map/attend/pallas_call | solution.py:320
  26.0 0.0 collective-permute-done.8.refs_7_
  26.0 0.1 collective-permute-start.11
  26.1 1.6 %collective-permute-done.11.refs_8_ = bf16[3,3,128,128]{3,2,1,0:T(8,128)(2,1)S(1)} collective-permute-done((bf16[3,3,128,128]{3,2,1,0:T(8,128)(2,1)S(1)}, bf16[3,3,128,128]{3,2,1,0:T(8,128)(2,1)S(1)}, u32[]{:S(2)}, u32[]{:S(2)}) %collective-permute-start.11) | collective-permute-done | bytes 294944 | tf_op jit(solution)/shard_map/ppermute | solution.py:352
  27.6 5.5 %attend.3 = (bf16[512,256]{1,0:T(8,128)(2,1)}, bf16[512,256]{1,0:T(8,128)(2,1)}, bf16[512,256]{1,0:T(8,128)(2,1)}, bf16[3,2048,128]{2,1,0:T(8,128)(2,1)S(1)}) custom-call(s32[16]{0:T(128)S(1)} %copy-done.5, s32[16]{0:T(128)S(1)} %copy-done.6, bf16[3,2048,128]{2,1,0:T(8,128)(2,1)S(1)} %get-tuple-element.14.refs_0_, ...), custom_call_target="tpu_custom_call", output_to_operand_aliasing={{3}: (2, {})} | custom-call | flops 1000000 | bytes 10000 | tf_op jit(solution)/shard_map/attend/pallas_call | solution.py:320
Async XLA Ops:
  0.6 9.8 %copy-start = (bf16[512,256]{1,0:T(8,128)(2,1)S(1)}, bf16[512,256]{1,0:T(8,128)(2,1)}, u32[]{:S(2)}) copy-start(bf16[512,256]{1,0:T(8,128)(2,1)} %refs_1_.5) | copy-start | bytes 786436
  0.6 1.8 %collective-permute-start.1 = (bf16[512,256]{1,0:T(8,128)(2,1)}, bf16[512,256]{1,0:T(8,128)(2,1)S(1)}, u32[]{:S(2)}, u32[]{:S(2)}) collective-permute-start(bf16[512,256]{1,0:T(8,128)(2,1)} %refs_1_.3), channel_id=1, source_target_pairs={{0,4},{4,0},{8,12},{12,8},{1,5},{5,1},{9,13},{13,9},{2,6},{6,2},{1... | collective-permute-start | bytes 786440 | tf_op jit(solution)/shard_map/ppermute | solution.py:352
  0.7 2.1 %collective-permute-start = (bf16[512,256]{1,0:T(8,128)(2,1)}, bf16[512,256]{1,0:T(8,128)(2,1)S(1)}, u32[]{:S(2)}, u32[]{:S(2)}) collective-permute-start(bf16[512,256]{1,0:T(8,128)(2,1)} %refs_0_.1), channel_id=1, source_target_pairs={{0,4},{4,0},{8,12},{12,8},{1,5},{5,1},{9,13},{13,9},{2,6},{6,2},{1... | collective-permute-start | bytes 786440 | tf_op jit(solution)/shard_map/ppermute | solution.py:352
  1.2 2.0 %collective-permute-start.2 = (bf16[512,256]{1,0:T(8,128)(2,1)}, bf16[512,256]{1,0:T(8,128)(2,1)S(1)}, u32[]{:S(2)}, u32[]{:S(2)}) collective-permute-start(bf16[512,256]{1,0:T(8,128)(2,1)} %refs_2_.1), channel_id=1, source_target_pairs={{0,4},{4,0},{8,12},{12,8},{1,5},{5,1},{9,13},{13,9},{2,6},{6,2},{1... | collective-permute-start | bytes 786440 | tf_op jit(solution)/shard_map/ppermute | solution.py:352
  1.3 9.1 %collective-permute-start.4 = (bf16[512,256]{1,0:T(8,128)(2,1)}, bf16[512,256]{1,0:T(8,128)(2,1)S(1)}, u32[]{:S(2)}, u32[]{:S(2)}) collective-permute-start(bf16[512,256]{1,0:T(8,128)(2,1)} %refs_1_.5), channel_id=1, source_target_pairs={{0,8},{4,12},{8,0},{12,4},{1,9},{5,13},{9,1},{13,5},{2,10},{6,14},... | collective-permute-start | bytes 786440 | tf_op jit(solution)/shard_map/ppermute | solution.py:352
  3.2 1.0 %copy-start.1 = (bf16[512,256]{1,0:T(8,128)(2,1)S(1)}, bf16[512,256]{1,0:T(8,128)(2,1)}, u32[]{:S(2)}) copy-start(bf16[512,256]{1,0:T(8,128)(2,1)} %refs_0_.1) | copy-start | bytes 786436
  4.2 0.9 %copy-start.2 = (bf16[512,256]{1,0:T(8,128)(2,1)S(1)}, bf16[512,256]{1,0:T(8,128)(2,1)}, u32[]{:S(2)}) copy-start(bf16[512,256]{1,0:T(8,128)(2,1)} %refs_1_.3) | copy-start | bytes 786436
  5.1 0.9 %copy-start.3 = (bf16[512,256]{1,0:T(8,128)(2,1)S(1)}, bf16[512,256]{1,0:T(8,128)(2,1)}, u32[]{:S(2)}) copy-start(bf16[512,256]{1,0:T(8,128)(2,1)} %refs_2_.1) | copy-start | bytes 786436
  6.1 0.7 %copy-start.4 = (s32[16]{0:T(128)S(1)}, s32[16]{0:T(128)}, u32[]{:S(2)}) copy-start(s32[16]{0:T(128)} %order.5) | copy-start | bytes 196
  6.7 14.6 %copy-start.5 = (s32[16]{0:T(128)S(1)}, s32[16]{0:T(128)}, u32[]{:S(2)}) copy-start(s32[16]{0:T(128)} %order.5) | copy-start | bytes 196
  6.7 14.6 %copy-start.6 = (s32[16]{0:T(128)S(1)}, s32[16]{0:T(128)}, u32[]{:S(2)}) copy-start(s32[16]{0:T(128)} %docs.3) | copy-start | bytes 196
  7.8 7.8 %collective-permute-start.6 = (bf16[2,3,128,128]{3,2,1,0:T(8,128)(2,1)S(1)}, bf16[2,3,128,128]{3,2,1,0:T(8,128)(2,1)S(1)}, u32[]{:S(2)}, u32[]{:S(2)}) collective-permute-start(bf16[2,3,128,128]{3,2,1,0:T(8,128)(2,1)S(1)} %get-tuple-element.15), channel_id=1, source_target_pairs={{0,8},{4,12},{8,0},{12,4},{1,9},{5,13},{9,1},{13,5},{2,10},{6,14},... | collective-permute-start | bytes 589832 | tf_op jit(solution)/shard_map/ppermute | solution.py:352
  8.4 11.5 %collective-permute-start.9 = (bf16[2,3,128,128]{3,2,1,0:T(8,128)(2,1)S(1)}, bf16[2,3,128,128]{3,2,1,0:T(8,128)(2,1)S(1)}, u32[]{:S(2)}, u32[]{:S(2)}) collective-permute-start(bf16[2,3,128,128]{3,2,1,0:T(8,128)(2,1)S(1)} %get-tuple-element.18), channel_id=1, source_target_pairs={{0,8},{4,12},{8,0},{12,4},{1,9},{5,13},{9,1},{13,5},{2,10},{6,14},... | collective-permute-start | bytes 589832 | tf_op jit(solution)/shard_map/ppermute | solution.py:352
  9.9 16.1 %collective-permute-start.8 = (bf16[3,3,128,128]{3,2,1,0:T(8,128)(2,1)S(1)}, bf16[3,3,128,128]{3,2,1,0:T(8,128)(2,1)S(1)}, u32[]{:S(2)}, u32[]{:S(2)}) collective-permute-start(bf16[3,3,128,128]{3,2,1,0:T(8,128)(2,1)S(1)} %get-tuple-element.16), channel_id=1, source_target_pairs={{0,8},{4,12},{8,0},{12,4},{1,9},{5,13},{9,1},{13,5},{2,10},{6,14},... | collective-permute-start | bytes 884744 | tf_op jit(solution)/shard_map/ppermute | solution.py:352
  10.4 9.4 %collective-permute-start.3 = (bf16[512,256]{1,0:T(8,128)(2,1)S(1)}, bf16[512,256]{1,0:T(8,128)(2,1)S(1)}, u32[]{:S(2)}, u32[]{:S(2)}) collective-permute-start(bf16[512,256]{1,0:T(8,128)(2,1)S(1)} %copy-done), channel_id=1, source_target_pairs={{0,4},{4,0},{8,12},{12,8},{1,5},{5,1},{9,13},{13,9},{2,6},{6,2},{1... | collective-permute-start | bytes 786440 | tf_op jit(solution)/shard_map/ppermute | solution.py:352
  10.4 9.4 %collective-permute-start.5 = (bf16[512,256]{1,0:T(8,128)(2,1)S(1)}, bf16[512,256]{1,0:T(8,128)(2,1)S(1)}, u32[]{:S(2)}, u32[]{:S(2)}) collective-permute-start(bf16[512,256]{1,0:T(8,128)(2,1)S(1)} %collective-permute-done.4.refs_3_), channel_id=1, source_target_pairs={{0,4},{4,0},{8,12},{12,8},{1,5},{5,1},{9,13},{13,9},{2,6},{6,2},{1... | collective-permute-start | bytes 786440 | tf_op jit(solution)/shard_map/ppermute | solution.py:352
  15.6 4.2 %collective-permute-start.7 = (bf16[2,3,128,128]{3,2,1,0:T(8,128)(2,1)S(1)}, bf16[2,3,128,128]{3,2,1,0:T(8,128)(2,1)S(1)}, u32[]{:S(2)}, u32[]{:S(2)}) collective-permute-start(bf16[2,3,128,128]{3,2,1,0:T(8,128)(2,1)S(1)} %collective-permute-done.6.refs_5_.refs_8_), channel_id=1, source_target_pairs={{0,4},{4,0},{8,12},{12,8},{1,5},{5,1},{9,13},{13,9},{2,6},{6,2},{1... | collective-permute-start | bytes 589832 | tf_op jit(solution)/shard_map/ppermute | solution.py:352
  19.8 1.4 %collective-permute-start.10 = (bf16[2,3,128,128]{3,2,1,0:T(8,128)(2,1)S(1)}, bf16[2,3,128,128]{3,2,1,0:T(8,128)(2,1)S(1)}, u32[]{:S(2)}, u32[]{:S(2)}) collective-permute-start(bf16[2,3,128,128]{3,2,1,0:T(8,128)(2,1)S(1)} %collective-permute-done.9.refs_7_), channel_id=1, source_target_pairs={{0,4},{4,0},{8,12},{12,8},{1,5},{5,1},{9,13},{13,9},{2,6},{6,2},{1... | collective-permute-start | bytes 589832 | tf_op jit(solution)/shard_map/ppermute | solution.py:352
  26.0 1.6 %collective-permute-start.11 = (bf16[3,3,128,128]{3,2,1,0:T(8,128)(2,1)S(1)}, bf16[3,3,128,128]{3,2,1,0:T(8,128)(2,1)S(1)}, u32[]{:S(2)}, u32[]{:S(2)}) collective-permute-start(bf16[3,3,128,128]{3,2,1,0:T(8,128)(2,1)S(1)} %collective-permute-done.8.refs_7_), channel_id=1, source_target_pairs={{0,4},{4,0},{8,12},{12,8},{1,5},{5,1},{9,13},{13,9},{2,6},{6,2},{1... | collective-permute-start | bytes 884744 | tf_op jit(solution)/shard_map/ppermute | solution.py:352
